TPU v7x, 32 devices: a whole 2x2x4 slice. The times are simulated.
32 devices in a mesh: tile: 8 (over z, x), dp: 4 (over y, core).
Axes of the slice: x: 2, y: 2, z: 4, core: 2. Of those that a mesh axis runs over, the one named last changes fastest.
Arguments:
- fields: bfloat16 [4, 16, 64, 64, 128], P('dp', 'tile'), may hold values from -6 to 6
- cotangent: bfloat16 [4, 16, 64, 64, 128], P('dp', 'tile'), may hold values from -6 to 6
- is_ocean: int32 [16], P('tile'), may hold values from 0 to 1, as said below
- neighbours: int32 [16, 8], P('tile'), may hold values from -1 to 15, as said below
- kernel: float32 [7, 7, 128], replicated, may hold values from -0.875 to 0.875
- conv_bias: float32 [128], replicated, may hold values from -3 to 3
- ln_gain: float32 [128], replicated, may hold values from 0.25 to 1.75
- ln_bias: float32 [128], replicated, may hold values from -3 to 3
- w_up: bfloat16 [128, 512], replicated, may hold values from -0.5 to 0.5
- up_bias: float32 [512], replicated, may hold values from -3 to 3
- w_down: bfloat16 [512, 128], replicated, may hold values from -0.25 to 0.25
- down_bias: float32 [128], replicated, may hold values from -3 to 3
- layer_scale: float32 [128], replicated, may hold values from 0.3 to 1
Outputs:
- grad_fields: bfloat16 [4, 16, 64, 64, 128], P('dp', 'tile')
- g_kernel: float32 [7, 7, 128], replicated
- g_conv_bias: float32 [128], replicated
- g_ln_gain: float32 [128], replicated
- g_ln_bias: float32 [128], replicated
- g_w_up: float32 [128, 512], replicated
- g_up_bias: float32 [512], replicated
- g_w_down: float32 [512, 128], replicated
- g_down_bias: float32 [128], replicated
- g_layer_scale: float32 [128], replicated
Inputs may be any that keep to these rules, and one draw needn't show every extreme that they name: `is_ocean`: slots follow a serpentine curve through the columns of a grid of 8 x 2 tiles, alternating direction from column to column; tiles of the first and last grid rows are ocean. Entry k of slot s names the slot of the tile adjacent in direction k (north, south, west, east, north-west, north-east, south-west, south-east), or -1 where that tile is land or outside the grid or slot s is land; the relation is symmetric; the north and south neighbours are slot s - 1 or s + 1, and every neighbour lies within 15 slots of s.
All inputs are finite; a program needn't handle non-finite values.
Results may differ from a plain program's by a relative error of at most 0.0071.
Values may be sent and summed in bfloat16 or wider, within the bound.
A program may use at most 128 MiB of HBM per device.

v0:
```python
from functools import partial
import math

import jax
import jax.numpy as jnp
from jax import lax
from jax.sharding import PartitionSpec as P

TROWS = 8


EPSILON = 1e-06


def passed_along(value, axis, by):
    devices = lax.axis_size(axis)
    pairs = [(i, i + by) for i in range(devices) if 0 <= i + by < devices]
    return lax.ppermute(value, axis, pairs)


def partner(value, axis, stride):
    mask = 2**stride
    pairs = [(source, source ^ mask) for source in range(lax.axis_size(axis))]
    return lax.ppermute(value, axis, pairs)


def rims_of(tile_block, rim_depth):
    extent = tile_block.shape[0]
    top_band = tile_block[:rim_depth]
    bottom = tile_block[extent - rim_depth :]
    left_band = jnp.transpose(tile_block[:, :rim_depth], (1, 0, 2))
    right_band = jnp.transpose(tile_block[:, extent - rim_depth :], (1, 0, 2))
    return jnp.stack([top_band, bottom, left_band, right_band], 0)


def assemble(own_tile, picked, valid_flags, first_layer, rim_depth):
    extent = own_tile.shape[0]

    def rim_piece(direction, which_strip):
        stripe = picked[direction][which_strip, first_layer : first_layer + rim_depth]
        return stripe * valid_flags[direction].astype(own_tile.dtype)

    north_rim = rim_piece(0, 1)
    south_rim = rim_piece(1, 0)
    west_rim = jnp.transpose(rim_piece(2, 1), (1, 0, 2))
    east_rim = jnp.transpose(rim_piece(3, 0), (1, 0, 2))
    north_west = jnp.transpose(rim_piece(4, 1)[:, extent - rim_depth :], (1, 0, 2))
    north_east = jnp.transpose(rim_piece(5, 0)[:, extent - rim_depth :], (1, 0, 2))
    south_west = jnp.transpose(rim_piece(6, 1)[:, :rim_depth], (1, 0, 2))
    south_east = jnp.transpose(rim_piece(7, 0)[:, :rim_depth], (1, 0, 2))
    top_band = jnp.concatenate([north_west, north_rim, north_east], 1)
    middle = jnp.concatenate([west_rim, own_tile, east_rim], 1)
    bottom = jnp.concatenate([south_west, south_rim, south_east], 1)
    return jnp.concatenate([top_band, middle, bottom], 0)


def depthwise(padded, kernel, extent):
    running_sum = jnp.zeros((extent, extent, padded.shape[2]), jnp.float32)
    for lag_row in range(7):
        for lag_col in range(7):
            window = padded[lag_row : lag_row + extent, lag_col : lag_col + extent].astype(
                jnp.float32
            )
            running_sum = running_sum + window * kernel[lag_row, lag_col]
    return running_sum


def transposed(grad_padded, kernel, extent):
    running_sum = jnp.zeros((extent, extent, grad_padded.shape[2]), jnp.float32)
    for lag_row in range(7):
        for lag_col in range(7):
            window = grad_padded[
                6 - lag_row : 6 - lag_row + extent, 6 - lag_col : 6 - lag_col + extent
            ].astype(jnp.float32)
            running_sum = running_sum + window * kernel[lag_row, lag_col]
    return running_sum


def kernel_terms(grad_tile, padded, extent):
    grad_values = grad_tile.astype(jnp.float32)
    stacked = []
    for lag_row in range(7):
        line_terms = []
        for lag_col in range(7):
            window = padded[lag_row : lag_row + extent, lag_col : lag_col + extent].astype(
                jnp.float32
            )
            line_terms.append(jnp.sum(grad_values * window, axis=(0, 1)))
        stacked.append(jnp.stack(line_terms, 0))
    return jnp.stack(stacked, 0)


def gelu_tanh(values):
    return jax.nn.gelu(values, approximate=True)


def contract_last(left_rows, right_matrix):
    return lax.dot_general(
        left_rows, right_matrix, (((1,), (1,)), ((), ())), preferred_element_type=jnp.float32
    )


def contract_first(left_rows, right_rows):
    return lax.dot_general(
        left_rows, right_rows, (((0,), (0,)), ((), ())), preferred_element_type=jnp.float32
    )


def layer_rows(
    conv_rows, cot_rows, ln_gain, ln_bias, w_up, up_bias, w_down, down_bias, layer_scale
):
    mean_value = jnp.mean(conv_rows, -1, keepdims=True)
    centred = conv_rows - mean_value
    variance = jnp.mean(centred * centred, -1, keepdims=True)
    inverse_scale = lax.rsqrt(variance + EPSILON)
    normed = centred * inverse_scale
    scaled = (normed * ln_gain + ln_bias).astype(jnp.bfloat16)
    hidden_sum = jnp.dot(scaled, w_up, preferred_element_type=jnp.float32) + up_bias
    activation = gelu_tanh(hidden_sum).astype(jnp.bfloat16)
    mixed = jnp.dot(activation, w_down, preferred_element_type=jnp.float32) + down_bias
    grad_mixed = (cot_rows * layer_scale).astype(jnp.bfloat16)
    grad_act = contract_last(grad_mixed, w_down)
    pullback = jax.vjp(gelu_tanh, hidden_sum)[1]
    grad_pre = pullback(grad_act)[0].astype(jnp.bfloat16)
    grad_scaled = contract_last(grad_pre, w_up)
    grad_normed = grad_scaled * ln_gain
    grad_conv = inverse_scale * (
        grad_normed
        - jnp.mean(grad_normed, -1, keepdims=True)
        - normed * jnp.mean(grad_normed * normed, -1, keepdims=True)
    )
    return (
        grad_conv.astype(jnp.bfloat16),
        mixed,
        grad_mixed,
        activation,
        grad_pre,
        scaled,
        grad_scaled,
        normed,
    )


def row_terms(
    cot_rows, mixed, grad_mixed, activation, grad_pre, scaled, grad_scaled, normed, grad_conv
):
    return (
        jnp.sum(grad_conv.astype(jnp.float32), 0),
        jnp.sum(grad_scaled * normed, 0),
        jnp.sum(grad_scaled, 0),
        contract_first(scaled, grad_pre),
        jnp.sum(grad_pre.astype(jnp.float32), 0),
        contract_first(activation, grad_mixed),
        jnp.sum(grad_mixed.astype(jnp.float32), 0),
        jnp.sum(cot_rows * mixed, 0),
    )


def local(
    fields,
    cotangent,
    is_ocean,
    neighbours,
    kernel,
    conv_bias,
    ln_gain,
    ln_bias,
    w_up,
    up_bias,
    w_down,
    down_bias,
    layer_scale,
):
    samples, slot_count, extent, channels = (
        fields.shape[0],
        fields.shape[1],
        fields.shape[2],
        fields.shape[4],
    )
    hidden_width = w_up.shape[1]
    tile_count = lax.axis_size("tile")
    position = lax.axis_index("tile")
    vert_base = (position - 1) * slot_count
    layer_params = (ln_gain, ln_bias, w_up, up_bias, w_down, down_bias, layer_scale)
    zero_terms = (
        jnp.zeros((7, 7, channels), jnp.float32),
        jnp.zeros((channels,), jnp.float32),
        jnp.zeros((channels,), jnp.float32),
        jnp.zeros((channels,), jnp.float32),
        jnp.zeros((channels, hidden_width), jnp.float32),
        jnp.zeros((hidden_width,), jnp.float32),
        jnp.zeros((hidden_width, channels), jnp.float32),
        jnp.zeros((channels,), jnp.float32),
        jnp.zeros((channels,), jnp.float32),
    )

    def collect(rim_set):
        adjacent = {}
        for offset in (1, -1):
            adjacent[offset] = passed_along(rim_set, "tile", offset)
        vertical = jnp.concatenate([adjacent[1], rim_set, adjacent[-1]], 1)
        per_column = TROWS // slot_count
        band = vertical[:, :, 2:4]
        west_band = passed_along(band, "tile", per_column)
        east_band = passed_along(band, "tile", -per_column)
        for bit_number in range(per_column.bit_length() - 1):
            west_band, east_band = partner((west_band, east_band), "tile", bit_number)
        sideways = jnp.concatenate([west_band, east_band], 1)
        row_within = position % per_column
        column_id = position // per_column
        west_device = (column_id - 1) * per_column + per_column - 1 - row_within
        east_device = (column_id + 1) * per_column + per_column - 1 - row_within
        west_start = (west_device - 1) * slot_count
        east_start = (east_device - 1) * slot_count - 3 * slot_count
        bases = jnp.stack([west_start, east_start, west_start, east_start, west_start, east_start])
        return (vertical, sideways, bases)

    def fetch_rims(vertical, sideways, bases, slot_ids):
        upright = jnp.clip(slot_ids[:2] - vert_base, 0, vertical.shape[0] - 1)
        lateral = jnp.clip(slot_ids[2:] - bases, 0, sideways.shape[0] - 1)
        picked = [vertical[upright[0]], vertical[upright[1]]]
        picked = picked + [sideways[lateral[slot_pick]] for slot_pick in range(6)]
        return (picked, slot_ids >= 0)

    grad_sums = zero_terms
    rims_x = jax.vmap(jax.vmap(partial(rims_of, rim_depth=3)))(fields)
    vertical_x, sideways_x, bases_x = collect(rims_x)
    sample = 0
    tile_stack = fields[sample]
    cot_stack = cotangent[sample]

    def first_work(slot_id):
        picked, valid_flags = fetch_rims(
            vertical_x[sample], sideways_x[sample], bases_x, neighbours[slot_id]
        )
        padded = assemble(tile_stack[slot_id], picked, valid_flags, 0, 3)
        conv_out = depthwise(padded, kernel, extent) + conv_bias
        cot_rows = cot_stack[slot_id].astype(jnp.float32).reshape(-1, channels)
        layer_parts = layer_rows(conv_out.reshape(-1, channels), cot_rows, *layer_params)
        grad_tile = layer_parts[0].reshape(extent, extent, channels)
        weight_terms = (kernel_terms(grad_tile, padded, extent),) + row_terms(
            cot_rows, *layer_parts[1:], layer_parts[0]
        )
        keep_flag = (is_ocean[slot_id] > 0).astype(jnp.float32)
        return (grad_tile, tuple((keep_flag * term for term in weight_terms)))

    def first_step(running, slot_id):
        grad_tile, weight_terms = first_work(slot_id)
        return (tuple((total + term for total, term in zip(running, weight_terms))), grad_tile)

    grad_sums, sample_grads = lax.scan(first_step, grad_sums, jnp.arange(slot_count))
    grad_tiles = [sample_grads]
    grad_stack = jnp.stack(grad_tiles, 0)
    rims_g = jax.vmap(jax.vmap(partial(rims_of, rim_depth=3)))(grad_stack)
    vertical_g, sideways_g, bases_g = collect(rims_g)
    sample = 0
    cot_stack = cotangent[sample]

    def second_step(slot_id):
        picked, valid_flags = fetch_rims(
            vertical_g[sample], sideways_g[sample], bases_g, neighbours[slot_id]
        )
        grad_padded = assemble(grad_stack[sample, slot_id], picked, valid_flags, 0, 3)
        result = cot_stack[slot_id].astype(jnp.float32) + transposed(grad_padded, kernel, extent)
        keep_flag = (is_ocean[slot_id] > 0).astype(jnp.float32)
        return (result * keep_flag).astype(jnp.bfloat16)

    outputs = [lax.map(second_step, jnp.arange(slot_count))]
    summed = lax.psum(
        (
            grad_sums[0],
            grad_sums[1],
            grad_sums[2],
            grad_sums[3],
            grad_sums[4],
            grad_sums[5],
            grad_sums[6],
            grad_sums[7],
            grad_sums[8],
        ),
        ("tile", "dp"),
    )
    grad_scale = 1.0 / math.sqrt(
        samples * lax.axis_size("dp") * slot_count * tile_count * extent * extent
    )
    return (
        jnp.stack(outputs, 0),
        summed[0] * grad_scale,
        summed[1] * grad_scale,
        summed[2] * grad_scale,
        summed[3] * grad_scale,
        summed[4] * grad_scale,
        summed[5] * grad_scale,
        summed[6] * grad_scale,
        summed[7] * grad_scale,
        summed[8] * grad_scale,
    )


def solution(mesh):
    placed = (
        P("dp", "tile", None, None, None),
        P("dp", "tile", None, None, None),
        P("tile"),
        P("tile", None),
        P(),
        P(),
        P(),
        P(),
        P(),
        P(),
        P(),
        P(),
        P(),
    )
    return jax.shard_map(
        local,
        mesh=mesh,
        in_specs=placed,
        out_specs=(P("dp", "tile", None, None, None), P(), P(), P(), P(), P(), P(), P(), P(), P()),
        check_vma=False,
    )
```

profile of v0, /device:TPU:0, one launch (start us, length us, event | category | flops | bytes accessed | tf_op | source)
XLA Modules:
  0.0 589.6 jit_solution(12477053132144172568)
XLA Ops:
  9.4 1.3 collective-permute-start.1
  10.7 5.5 collective-permute-start
  16.2 7.2 %collective-permute-done.1 = bf16[1,2,4,3,64,128]{5,4,3,2,1,0:T(8,128)(2,1)S(1)} collective-permute-done((bf16[1,2,4,3,64,128]{5,4,3,2,1,0:T(8,128)(2,1)S(1)}, bf16[1,2,4,3,64,128]{5,4,3,2,1,0:T(8,128)(2,1)S(1)}, u32[]{:S(2)}, u32[]{:S(2)}) %collective-permute-start.1) | collective-permute-done | bytes 393248 | tf_op jit(solution)/shard_map/ppermute | solution.py:18
  23.4 8.6 %collective-permute-done = bf16[1,2,4,3,64,128]{5,4,3,2,1,0:T(8,128)(2,1)S(1)} collective-permute-done((bf16[1,2,4,3,64,128]{5,4,3,2,1,0:T(8,128)(2,1)S(1)}, bf16[1,2,4,3,64,128]{5,4,3,2,1,0:T(8,128)(2,1)S(1)}, u32[]{:S(2)}, u32[]{:S(2)}) %collective-permute-start) | collective-permute-done | bytes 393248 | tf_op jit(solution)/shard_map/ppermute | solution.py:18
  34.2 1.3 collective-permute-start.5
  35.5 5.5 collective-permute-start.2
  41.1 23.9 %collective-permute-done.5 = bf16[1,6,2,3,64,128]{5,4,3,2,1,0:T(8,128)(2,1)S(1)} collective-permute-done((bf16[1,6,2,3,64,128]{5,4,3,2,1,0:T(8,128)(2,1)S(1)}, bf16[1,6,2,3,64,128]{5,4,3,2,1,0:T(8,128)(2,1)S(1)}, u32[]{:S(2)}, u32[]{:S(2)}) %collective-permute-start.5) | collective-permute-done | bytes 589856 | tf_op jit(solution)/shard_map/ppermute | solution.py:18
  64.9 2.5 collective-permute-start.6
  67.4 14.3 %collective-permute-done.6 = bf16[1,6,2,3,64,128]{5,4,3,2,1,0:T(8,128)(2,1)} collective-permute-done((bf16[1,6,2,3,64,128]{5,4,3,2,1,0:T(8,128)(2,1)S(1)}, bf16[1,6,2,3,64,128]{5,4,3,2,1,0:T(8,128)(2,1)}, u32[]{:S(2)}, u32[]{:S(2)}) %collective-permute-start.6) | collective-permute-done | bytes 589856 | tf_op jit(solution)/shard_map/ppermute | solution.py:24
  81.8 11.1 %collective-permute-done.3 = bf16[1,6,2,3,64,128]{5,4,3,2,1,0:T(8,128)(2,1)} collective-permute-done((bf16[1,6,2,3,64,128]{5,4,3,2,1,0:T(8,128)(2,1)S(1)}, bf16[1,6,2,3,64,128]{5,4,3,2,1,0:T(8,128)(2,1)}, u32[]{:S(2)}, u32[]{:S(2)}) %collective-permute-start.3) | collective-permute-done | bytes 589856 | tf_op jit(solution)/shard_map/ppermute | solution.py:24
  94.2 12.6 %collective-permute-done.4 = bf16[1,6,2,3,64,128]{5,4,3,2,1,0:T(8,128)(2,1)S(1)} collective-permute-done((bf16[1,6,2,3,64,128]{5,4,3,2,1,0:T(8,128)(2,1)}, bf16[1,6,2,3,64,128]{5,4,3,2,1,0:T(8,128)(2,1)S(1)}, u32[]{:S(2)}, u32[]{:S(2)}) %collective-permute-start.4) | collective-permute-done | bytes 589856 | tf_op jit(solution)/shard_map/ppermute | solution.py:24
  106.9 2.3 copy.32
  109.6 214.0 %while.42 = (s32[]{:T(128)}, f32[7,7,128]{2,1,0:T(8,128)}, f32[128]{0:T(128)}, f32[128]{0:T(128)}, f32[128]{0:T(128)}, /*index=5*/f32[128,512]{1,0:T(8,128)}, f3...) while((s32[]{:T(128)}, f32[7,7,128]{2,1,0:T(8,128)}, ...), condition=%wide.region_60.61_spmd.clone, body=%wide.region_0.60_spmd.clone.sunk | while | flops 3501007872 | bytes 225164176 | solution.py:251
  145.5 1.7 dynamic-slice_convert_fusion.2
  147.2 3.2 maximum_maximum_fusion.7
  150.4 17.6 %fusion.226 = (f32[64,64]{1,0:T(8,128)S(1)}, f32[64,64,128]{2,1,0:T(8,128)}) fusion(f32[128]{0:T(128)} %get-tuple-element.1748, f32[128]{0:T(128)S(1)} %get-tuple-element.1543, bf16[67,70,128]{2,1,0:T(8,128)(2,1)S(1)} %get-tuple-element.1542, f32[128]{0:T(128)S(1)} %get-tuple-element.1544, f32[128]{0:T(128)S(1)} %get-tuple-element.1545, ...), kind=kLoop, calls=%fused_computation.461.clone.1 | loop fusion | flops 87027712 | bytes 47326208 | tf_op jit(solution)/shard_map/while/body/eval_jaxpr/reduce_sum | solution.py:112
  168.7 2.5 multiply_reduce_fusion.6
  172.7 4.4 add_convert_fusion.2
  177.1 3.3 multiply_convert_fusion.5
  180.4 1.3 fusion.237
  181.8 6.7 %convert_reduce_fusion.6 = (f32[512]{0:T(512)S(1)}, bf16[4096,512]{1,0:T(8,128)(2,1)S(1)}) fusion(f32[4096,512]{1,0:T(8,128)S(1)} %get-tuple-element.1595, f32[512]{0:T(512)S(1)} %copy-done.72, bf16[4096,128]{1,0:T(8,128)(2,1)S(1)} %fusion.227, bf16[512,128]{1,0:T(8,128)(2,1)S(1)} %copy-done.16), kind=kOutput, calls=%fused_computation.106.clone.1 | convolution fusion | flops 585104896 | bytes 13766656 | tf_op jit(solution)/shard_map/while/body/eval_jaxpr/dot_general | solution.py:98
  188.5 1.3 fusion.235
  191.6 2.6 multiply_reduce_fusion.7
  194.3 8.9 %fusion.228 = (f32[128]{0:T(128)S(1)}, f32[128]{0:T(128)}, f32[128]{0:T(128)}, f32[128]{0:T(128)}, f32[128]{0:T(128)}, /*index=5*/f32[128]{0:T(128)}, f32[128]{0...) fusion(bf16[67,70,128]{2,1,0:T(8,128)(2,1)S(1)} %get-tuple-elem, ...), kind=kLoop, calls=%fused_computation.300.clone.1 | loop fusion | flops 33027840 | bytes 24192512 | tf_op jit(solution)/shard_map/while/body/eval_jaxpr/reduce_sum | solution.py:88
  203.2 4.7 fusion.229
  207.9 5.2 fusion.230
  214.6 1.7 copy_dynamic-update-slice_fusion.2
  252.8 1.7 dynamic-slice_convert_fusion.2
  254.5 3.2 maximum_maximum_fusion.7
  257.7 17.6 %fusion.226 = (f32[64,64]{1,0:T(8,128)S(1)}, f32[64,64,128]{2,1,0:T(8,128)}) fusion(f32[128]{0:T(128)} %get-tuple-element.1748, f32[128]{0:T(128)S(1)} %get-tuple-element.1543, bf16[67,70,128]{2,1,0:T(8,128)(2,1)S(1)} %get-tuple-element.1542, f32[128]{0:T(128)S(1)} %get-tuple-element.1544, f32[128]{0:T(128)S(1)} %get-tuple-element.1545, ...), kind=kLoop, calls=%fused_computation.461.clone.1 | loop fusion | flops 87027712 | bytes 47326208 | tf_op jit(solution)/shard_map/while/body/eval_jaxpr/reduce_sum | solution.py:112
  276.0 2.5 multiply_reduce_fusion.6
  280.0 4.4 add_convert_fusion.2
  284.4 3.3 multiply_convert_fusion.5
  287.7 1.3 fusion.237
  289.1 6.7 %convert_reduce_fusion.6 = (f32[512]{0:T(512)S(1)}, bf16[4096,512]{1,0:T(8,128)(2,1)S(1)}) fusion(f32[4096,512]{1,0:T(8,128)S(1)} %get-tuple-element.1595, f32[512]{0:T(512)S(1)} %copy-done.72, bf16[4096,128]{1,0:T(8,128)(2,1)S(1)} %fusion.227, bf16[512,128]{1,0:T(8,128)(2,1)S(1)} %copy-done.16), kind=kOutput, calls=%fused_computation.106.clone.1 | convolution fusion | flops 585104896 | bytes 13766656 | tf_op jit(solution)/shard_map/while/body/eval_jaxpr/dot_general | solution.py:98
  295.8 1.3 fusion.235
  298.9 2.6 multiply_reduce_fusion.7
  301.6 8.9 %fusion.228 = (f32[128]{0:T(128)S(1)}, f32[128]{0:T(128)}, f32[128]{0:T(128)}, f32[128]{0:T(128)}, f32[128]{0:T(128)}, /*index=5*/f32[128]{0:T(128)}, f32[128]{0...) fusion(bf16[67,70,128]{2,1,0:T(8,128)(2,1)S(1)} %get-tuple-elem, ...), kind=kLoop, calls=%fused_computation.300.clone.1 | loop fusion | flops 33027840 | bytes 24192512 | tf_op jit(solution)/shard_map/while/body/eval_jaxpr/reduce_sum | solution.py:88
  310.5 4.7 fusion.229
  315.2 5.2 fusion.230
  321.9 1.7 copy_dynamic-update-slice_fusion.2
  326.0 1.3 collective-permute-start.9
  327.3 5.3 collective-permute-start.8
  332.7 46.5 %all-reduce = (f32[7,7,128]{2,1,0:T(8,128)S(1)}, f32[128]{0:T(128)S(1)}, f32[128]{0:T(128)S(1)}, f32[128]{0:T(128)S(1)}, f32[512]{0:T(512)S(1)}, /*index=5*/f32[128]{0:T(128)S(1)}, f32[128]{0:T(128)S(1)}) all-reduce(f32[7,7,128]{2,1,0:T(8,128)S(1)} %copy-done.21, ...), channel_id=1, replica_groups=mesh['tile'=8,'dp'=4] {'tile','dp'}, use_global_device_ids=true, to_apply=%region_63.64 | all-reduce | flops 7424 | bytes 59392 | tf_op jit(solution)/shard_map/psum | solution.py:269
  379.9 1.4 pad_maximum_fusion.6
  382.6 5.5 collective-permute-start.10
  389.8 21.9 %collective-permute-done.13 = bf16[1,6,2,3,64,128]{5,4,3,2,1,0:T(8,128)(2,1)S(1)} collective-permute-done((bf16[1,6,2,3,64,128]{5,4,3,2,1,0:T(8,128)(2,1)S(1)}, bf16[1,6,2,3,64,128]{5,4,3,2,1,0:T(8,128)(2,1)S(1)}, u32[]{:S(2)}, u32[]{:S(2)}) %collective-permute-start.13) | collective-permute-done | bytes 589856 | tf_op jit(solution)/shard_map/ppermute | solution.py:18
  412.2 1.5 collective-permute-start.11
  415.3 12.6 %collective-permute-done.14 = bf16[1,6,2,3,64,128]{5,4,3,2,1,0:T(8,128)(2,1)} collective-permute-done((bf16[1,6,2,3,64,128]{5,4,3,2,1,0:T(8,128)(2,1)S(1)}, bf16[1,6,2,3,64,128]{5,4,3,2,1,0:T(8,128)(2,1)}, u32[]{:S(2)}, u32[]{:S(2)}) %collective-permute-start.14) | collective-permute-done | bytes 589856 | tf_op jit(solution)/shard_map/ppermute | solution.py:24
  428.0 12.1 %collective-permute-done.11 = bf16[1,6,2,3,64,128]{5,4,3,2,1,0:T(8,128)(2,1)} collective-permute-done((bf16[1,6,2,3,64,128]{5,4,3,2,1,0:T(8,128)(2,1)S(1)}, bf16[1,6,2,3,64,128]{5,4,3,2,1,0:T(8,128)(2,1)}, u32[]{:S(2)}, u32[]{:S(2)}) %collective-permute-start.11) | collective-permute-done | bytes 589856 | tf_op jit(solution)/shard_map/ppermute | solution.py:24
  440.6 31.4 %all-reduce.4.cloned.1.call-done = (f32[128,512]{1,0:T(8,128)}, f32[512,128]{1,0:T(8,128)}) async-done(((f32[128,512]{1,0:T(8,128)}, f32[512,128]{1,0:T(8,128)}), (f32[128,512]{1,0:T(8,128)}, f32[512,128]{1,0:T(8,128)})) %all-reduce.4.cloned.1.call-update) | async-done | bytes 524304 | tf_op jit(solution)/shard_map/psum | solution.py:269
  472.0 1.7 broadcast_multiply_fusion.4
  473.7 1.7 broadcast_multiply_fusion.3
  475.4 1.3 pad_maximum_fusion.7
  476.7 2.2 copy.37
  479.0 103.8 %while.41 = (s32[]{:T(128)}, bf16[2,64,64,128]{3,2,1,0:T(8,128)(2,1)}, s32[2]{0:T(128)S(1)}, bf16[2,64,64,128]{3,2,1,0:T(8,128)(2,1)S(1)}, s32[2,8]{1,0:T(2,128)...) while((s32[]{:T(128)}, ...), condition=%wide.region_62.63_spmd, body=%wide.region_61.62_spmd.sunk | while | flops 102684736 | bytes 72825256 | solution.py:268
  508.1 1.3 constant_dynamic-slice_fusion.7
  510.1 3.3 maximum_maximum_fusion.6
  513.4 16.1 %bitcast_dynamic-update-slice_fusion.2 = bf16[2,64,64,128]{3,2,1,0:T(8,128)(2,1)S(1)} fusion(bf16[2,64,64,128]{3,2,1,0:T(8,128)(2,1)S(1)} %copy-done.69, s32[]{:T(128)S(6)} %copy.96, f32[]{:T(128)} %bitcast.631, f32[128]{0:T(128)S(1)} %get-tuple-element.1401, bf16[67,70,128]{2,1,0:T(8,128)(2,1)S(1)} %get-tuple-element.1432, ...), kind=kLoop, calls=%fused_computation.20.clone.1 | loop fusion | flops 88080384 | bytes 47342092 | tf_op jit(solution)/shard_map/while/body/jit(dynamic_update_index_in_dim)/dynamic_update_slice | solution.py:251
  529.5 1.3 copy-done.70
  560.0 1.3 constant_dynamic-slice_fusion.7
  562.0 3.3 maximum_maximum_fusion.6
  565.3 16.1 %bitcast_dynamic-update-slice_fusion.2 = bf16[2,64,64,128]{3,2,1,0:T(8,128)(2,1)S(1)} fusion(bf16[2,64,64,128]{3,2,1,0:T(8,128)(2,1)S(1)} %copy-done.69, s32[]{:T(128)S(6)} %copy.96, f32[]{:T(128)} %bitcast.631, f32[128]{0:T(128)S(1)} %get-tuple-element.1401, bf16[67,70,128]{2,1,0:T(8,128)(2,1)S(1)} %get-tuple-element.1432, ...), kind=kLoop, calls=%fused_computation.20.clone.1 | loop fusion | flops 88080384 | bytes 47342092 | tf_op jit(solution)/shard_map/while/body/jit(dynamic_update_index_in_dim)/dynamic_update_slice | solution.py:251
  581.4 1.3 copy-done.70
  (444 shorter events, 66.4 us)
Async XLA Ops:
  7.2 464.8 %all-reduce.4.cloned.1.call-start = ((), (), s32[]{:S(2)}) async-start(), calls=%async_computation | async-start | bytes 1048576 | tf_op jit(solution)/shard_map/psum | solution.py:269
  9.4 14.0 %collective-permute-start.1 = (bf16[1,2,4,3,64,128]{5,4,3,2,1,0:T(8,128)(2,1)S(1)}, bf16[1,2,4,3,64,128]{5,4,3,2,1,0:T(8,128)(2,1)S(1)}, u32[]{:S(2)}, u32[]{:S(2)}) collective-permute-start(bf16[1,2,4,3,64,128]{5,4,3,2,1,0:T(8,128)(2,1)S(1)} %maximum_bitcast_fusion), channel_id=1, source_target_pairs={{4,0},{8,4},{12,8},{16,12},{20,16},{24,20},{28,24},{5,1},{9,5},{13... | collective-permute-start | bytes 1179656 | tf_op jit(solution)/shard_map/ppermute | solution.py:18
  10.7 21.2 %collective-permute-start = (bf16[1,2,4,3,64,128]{5,4,3,2,1,0:T(8,128)(2,1)S(1)}, bf16[1,2,4,3,64,128]{5,4,3,2,1,0:T(8,128)(2,1)S(1)}, u32[]{:S(2)}, u32[]{:S(2)}) collective-permute-start(bf16[1,2,4,3,64,128]{5,4,3,2,1,0:T(8,128)(2,1)S(1)} %maximum_bitcast_fusion), channel_id=1, source_target_pairs={{0,4},{4,8},{8,12},{12,16},{16,20},{20,24},{24,28},{1,5},{5,9},{9,... | collective-permute-start | bytes 1179656 | tf_op jit(solution)/shard_map/ppermute | solution.py:18
  34.2 30.7 %collective-permute-start.5 = (bf16[1,6,2,3,64,128]{5,4,3,2,1,0:T(8,128)(2,1)S(1)}, bf16[1,6,2,3,64,128]{5,4,3,2,1,0:T(8,128)(2,1)S(1)}, u32[]{:S(2)}, u32[]{:S(2)}) collective-permute-start(bf16[1,6,2,3,64,128]{5,4,3,2,1,0:T(8,128)(2,1)S(1)} %slice.1607), channel_id=1, source_target_pairs={{16,0},{20,4},{24,8},{28,12},{17,1},{21,5},{25,9},{29,13},{18,2},{... | collective-permute-start | bytes 1769480 | tf_op jit(solution)/shard_map/ppermute | solution.py:18
  35.5 31.9 %collective-permute-start.2 = (bf16[1,6,2,3,64,128]{5,4,3,2,1,0:T(8,128)(2,1)S(1)}, bf16[1,6,2,3,64,128]{5,4,3,2,1,0:T(8,128)(2,1)S(1)}, u32[]{:S(2)}, u32[]{:S(2)}) collective-permute-start(bf16[1,6,2,3,64,128]{5,4,3,2,1,0:T(8,128)(2,1)S(1)} %slice.1607), channel_id=1, source_target_pairs={{0,16},{4,20},{8,24},{12,28},{1,17},{5,21},{9,25},{13,29},{2,18},{... | collective-permute-start | bytes 1769480 | tf_op jit(solution)/shard_map/ppermute | solution.py:18
  64.9 16.8 %collective-permute-start.6 = (bf16[1,6,2,3,64,128]{5,4,3,2,1,0:T(8,128)(2,1)S(1)}, bf16[1,6,2,3,64,128]{5,4,3,2,1,0:T(8,128)(2,1)}, u32[]{:S(2)}, u32[]{:S(2)}) collective-permute-start(bf16[1,6,2,3,64,128]{5,4,3,2,1,0:T(8,128)(2,1)S(1)} %collective-permute-done.5), channel_id=1, source_target_pairs={{0,4},{4,0},{8,12},{12,8},{16,20},{20,16},{24,28},{28,24},{1,5},{5... | collective-permute-start | bytes 1769480 | tf_op jit(solution)/shard_map/ppermute | solution.py:24
  67.4 25.4 %collective-permute-start.3 = (bf16[1,6,2,3,64,128]{5,4,3,2,1,0:T(8,128)(2,1)S(1)}, bf16[1,6,2,3,64,128]{5,4,3,2,1,0:T(8,128)(2,1)}, u32[]{:S(2)}, u32[]{:S(2)}) collective-permute-start(bf16[1,6,2,3,64,128]{5,4,3,2,1,0:T(8,128)(2,1)S(1)} %collective-permute-done.2), channel_id=1, source_target_pairs={{0,4},{4,0},{8,12},{12,8},{16,20},{20,16},{24,28},{28,24},{1,5},{5... | collective-permute-start | bytes 1769480 | tf_op jit(solution)/shard_map/ppermute | solution.py:24
  81.8 12.4 %collective-permute-start.7 = (bf16[1,6,2,3,64,128]{5,4,3,2,1,0:T(8,128)(2,1)}, bf16[1,6,2,3,64,128]{5,4,3,2,1,0:T(8,128)(2,1)S(1)}, u32[]{:S(2)}, u32[]{:S(2)}) collective-permute-start(bf16[1,6,2,3,64,128]{5,4,3,2,1,0:T(8,128)(2,1)} %collective-permute-done.6), channel_id=1, source_target_pairs={{0,8},{4,12},{8,0},{12,4},{16,24},{20,28},{24,16},{28,20},{1,9},{5... | collective-permute-start | bytes 1769480 | tf_op jit(solution)/shard_map/ppermute | solution.py:24
  92.8 14.0 %collective-permute-start.4 = (bf16[1,6,2,3,64,128]{5,4,3,2,1,0:T(8,128)(2,1)}, bf16[1,6,2,3,64,128]{5,4,3,2,1,0:T(8,128)(2,1)S(1)}, u32[]{:S(2)}, u32[]{:S(2)}) collective-permute-start(bf16[1,6,2,3,64,128]{5,4,3,2,1,0:T(8,128)(2,1)} %collective-permute-done.3), channel_id=1, source_target_pairs={{0,8},{4,12},{8,0},{12,4},{16,24},{20,28},{24,16},{28,20},{1,9},{5... | collective-permute-start | bytes 1769480 | tf_op jit(solution)/shard_map/ppermute | solution.py:24
  93.5 16.1 %copy-start.4 = (bf16[1,2,64,64,128]{4,3,2,1,0:T(8,128)(2,1)S(1)}, bf16[1,2,64,64,128]{4,3,2,1,0:T(8,128)(2,1)}, u32[]{:S(2)}) copy-start(bf16[1,2,64,64,128]{4,3,2,1,0:T(8,128)(2,1)} %param.18) | copy-start | bytes 6291460
  133.9 11.6 %copy-start.10 = (bf16[2,64,64,128]{3,2,1,0:T(8,128)(2,1)S(1)}, bf16[2,64,64,128]{3,2,1,0:T(8,128)(2,1)}, u32[]{:S(2)}) copy-start(bf16[2,64,64,128]{3,2,1,0:T(8,128)(2,1)} %get-tuple-element.1746) | copy-start | bytes 6291460 | tf_op jit(solution)/shard_map/while
  144.5 5.8 copy-start.6
  144.5 5.8 copy-start.8
  147.2 20.8 %copy-start.1 = (bf16[1,64,64,128]{3,2,1,0:T(8,128)(2,1)}, bf16[1,64,64,128]{3,2,1,0:T(8,128)(2,1)S(1)}, u32[]{:S(2)}) copy-start(bf16[1,64,64,128]{3,2,1,0:T(8,128)(2,1)S(1)} %get-tuple-element.1526) | copy-start | bytes 3145732 | tf_op jit(solution)/shard_map/while
  171.2 5.9 copy-start.72
  172.7 4.4 copy-start.71
  177.1 3.3 copy-start.3
  177.1 3.3 copy-start.16
  177.1 3.3 copy-start.44
  181.8 6.7 %copy-start.11 = (f32[512,128]{1,0:T(8,128)S(1)}, f32[512,128]{1,0:T(8,128)}, u32[]{:S(2)}) copy-start(f32[512,128]{1,0:T(8,128)} %get-tuple-element.1699) | copy-start | bytes 786436 | tf_op jit(solution)/shard_map/while
  189.8 4.3 copy-start.12
  191.4 2.8 copy-start.24
  194.2 9.0 %copy-start.64 = (f32[128]{0:T(128)}, f32[128]{0:T(128)S(1)}, u32[]{:S(2)}) copy-start(f32[128]{0:T(128)S(1)} %fusion.232) | copy-start | bytes 1540 | tf_op jit(solution)/shard_map/while
  194.3 8.9 %copy-start.61 = (f32[128]{0:T(128)}, f32[128]{0:T(128)S(1)}, u32[]{:S(2)}) copy-start(f32[128]{0:T(128)S(1)} %fusion.233) | copy-start | bytes 1540 | tf_op jit(solution)/shard_map/while
  194.3 8.9 %copy-start.2 = (bf16[1,64,64,128]{3,2,1,0:T(8,128)(2,1)S(1)}, bf16[1,64,64,128]{3,2,1,0:T(8,128)(2,1)}, u32[]{:S(2)}) copy-start(bf16[1,64,64,128]{3,2,1,0:T(8,128)(2,1)} %copy-done.1) | copy-start | bytes 3145732 | tf_op jit(solution)/shard_map/while
  194.3 8.9 %copy-start.7 = (bf16[64,3,128]{2,1,0:T(4,128)(2,1)S(1)}, bf16[64,3,128]{2,1,0:T(4,128)(2,1)}, u32[]{:S(2)}) copy-start(bf16[64,3,128]{2,1,0:T(4,128)(2,1)} %copy-done.6) | copy-start | bytes 147460 | tf_op jit(solution)/shard_map/while
  194.3 8.9 %copy-start.9 = (bf16[64,3,128]{2,1,0:T(4,128)(2,1)S(1)}, bf16[64,3,128]{2,1,0:T(4,128)(2,1)}, u32[]{:S(2)}) copy-start(bf16[64,3,128]{2,1,0:T(4,128)(2,1)} %copy-done.8) | copy-start | bytes 147460 | tf_op jit(solution)/shard_map/while
  213.4 2.9 copy-start.5
  241.2 11.6 %copy-start.10 = (bf16[2,64,64,128]{3,2,1,0:T(8,128)(2,1)S(1)}, bf16[2,64,64,128]{3,2,1,0:T(8,128)(2,1)}, u32[]{:S(2)}) copy-start(bf16[2,64,64,128]{3,2,1,0:T(8,128)(2,1)} %get-tuple-element.1746) | copy-start | bytes 6291460 | tf_op jit(solution)/shard_map/while
  251.8 5.8 copy-start.6
  251.8 5.8 copy-start.8
  254.5 20.8 %copy-start.1 = (bf16[1,64,64,128]{3,2,1,0:T(8,128)(2,1)}, bf16[1,64,64,128]{3,2,1,0:T(8,128)(2,1)S(1)}, u32[]{:S(2)}) copy-start(bf16[1,64,64,128]{3,2,1,0:T(8,128)(2,1)S(1)} %get-tuple-element.1526) | copy-start | bytes 3145732 | tf_op jit(solution)/shard_map/while
  278.5 5.9 copy-start.72
  280.0 4.4 copy-start.71
  284.4 3.3 copy-start.3
  284.4 3.3 copy-start.16
  284.4 3.3 copy-start.44
  289.1 6.7 %copy-start.11 = (f32[512,128]{1,0:T(8,128)S(1)}, f32[512,128]{1,0:T(8,128)}, u32[]{:S(2)}) copy-start(f32[512,128]{1,0:T(8,128)} %get-tuple-element.1699) | copy-start | bytes 786436 | tf_op jit(solution)/shard_map/while
  297.1 4.3 copy-start.12
  298.7 2.8 copy-start.24
  301.5 9.0 %copy-start.64 = (f32[128]{0:T(128)}, f32[128]{0:T(128)S(1)}, u32[]{:S(2)}) copy-start(f32[128]{0:T(128)S(1)} %fusion.232) | copy-start | bytes 1540 | tf_op jit(solution)/shard_map/while
  301.6 8.9 %copy-start.61 = (f32[128]{0:T(128)}, f32[128]{0:T(128)S(1)}, u32[]{:S(2)}) copy-start(f32[128]{0:T(128)S(1)} %fusion.233) | copy-start | bytes 1540 | tf_op jit(solution)/shard_map/while
  301.6 8.9 %copy-start.2 = (bf16[1,64,64,128]{3,2,1,0:T(8,128)(2,1)S(1)}, bf16[1,64,64,128]{3,2,1,0:T(8,128)(2,1)}, u32[]{:S(2)}) copy-start(bf16[1,64,64,128]{3,2,1,0:T(8,128)(2,1)} %copy-done.1) | copy-start | bytes 3145732 | tf_op jit(solution)/shard_map/while
  301.6 8.9 %copy-start.7 = (bf16[64,3,128]{2,1,0:T(4,128)(2,1)S(1)}, bf16[64,3,128]{2,1,0:T(4,128)(2,1)}, u32[]{:S(2)}) copy-start(bf16[64,3,128]{2,1,0:T(4,128)(2,1)} %copy-done.6) | copy-start | bytes 147460 | tf_op jit(solution)/shard_map/while
  301.6 8.9 %copy-start.9 = (bf16[64,3,128]{2,1,0:T(4,128)(2,1)S(1)}, bf16[64,3,128]{2,1,0:T(4,128)(2,1)}, u32[]{:S(2)}) copy-start(bf16[64,3,128]{2,1,0:T(4,128)(2,1)} %copy-done.8) | copy-start | bytes 147460 | tf_op jit(solution)/shard_map/while
  320.7 3.0 copy-start.5
  323.7 8.9 %copy-start.21 = (f32[7,7,128]{2,1,0:T(8,128)S(1)}, f32[7,7,128]{2,1,0:T(8,128)}, u32[]{:S(2)}) copy-start(f32[7,7,128]{2,1,0:T(8,128)} %get-tuple-element.1826) | copy-start | bytes 75268
  323.7 8.9 %copy-start.25 = (f32[512]{0:T(512)S(1)}, f32[512]{0:T(512)}, u32[]{:S(2)}) copy-start(f32[512]{0:T(512)} %get-tuple-element.1831) | copy-start | bytes 6148
  323.7 8.9 %copy-start.59 = (f32[128]{0:T(128)S(1)}, f32[128]{0:T(128)}, u32[]{:S(2)}) copy-start(f32[128]{0:T(128)} %get-tuple-element.1834) | copy-start | bytes 1540
  323.7 8.9 %copy-start.62 = (f32[128]{0:T(128)S(1)}, f32[128]{0:T(128)}, u32[]{:S(2)}) copy-start(f32[128]{0:T(128)} %get-tuple-element.1829) | copy-start | bytes 1540
  323.7 8.9 %copy-start.65 = (f32[128]{0:T(128)S(1)}, f32[128]{0:T(128)}, u32[]{:S(2)}) copy-start(f32[128]{0:T(128)} %get-tuple-element.1828) | copy-start | bytes 1540
  323.7 8.9 %copy-start.68 = (f32[128]{0:T(128)S(1)}, f32[128]{0:T(128)}, u32[]{:S(2)}) copy-start(f32[128]{0:T(128)} %get-tuple-element.1827) | copy-start | bytes 1540
  326.0 53.2 %copy-start.18 = (bf16[1,2,4,3,64,128]{5,4,3,2,1,0:T(8,128)(2,1)}, bf16[1,2,4,3,64,128]{5,4,3,2,1,0:T(8,128)(2,1)S(1)}, u32[]{:S(2)}) copy-start(bf16[1,2,4,3,64,128]{5,4,3,2,1,0:T(8,128)(2,1)S(1)} %maximum_bitcast_fusion.1) | copy-start | bytes 1179652
  326.0 53.2 %collective-permute-start.9 = (bf16[1,2,4,3,64,128]{5,4,3,2,1,0:T(8,128)(2,1)S(1)}, bf16[1,2,4,3,64,128]{5,4,3,2,1,0:T(8,128)(2,1)S(1)}, u32[]{:S(2)}, u32[]{:S(2)}) collective-permute-start(bf16[1,2,4,3,64,128]{5,4,3,2,1,0:T(8,128)(2,1)S(1)} %maximum_bitcast_fusion.1), channel_id=1, source_target_pairs={{4,0},{8,4},{12,8},{16,12},{20,16},{24,20},{28,24},{5,1},{9,5},{13... | collective-permute-start | bytes 1179656 | tf_op jit(solution)/shard_map/ppermute | solution.py:18
  327.3 52.6 %collective-permute-start.8 = (bf16[1,2,4,3,64,128]{5,4,3,2,1,0:T(8,128)(2,1)S(1)}, bf16[1,2,4,3,64,128]{5,4,3,2,1,0:T(8,128)(2,1)}, u32[]{:S(2)}, u32[]{:S(2)}) collective-permute-start(bf16[1,2,4,3,64,128]{5,4,3,2,1,0:T(8,128)(2,1)S(1)} %maximum_bitcast_fusion.1), channel_id=1, source_target_pairs={{0,4},{4,8},{8,12},{12,16},{16,20},{20,24},{24,28},{1,5},{5,9},{9,... | collective-permute-start | bytes 1179656 | tf_op jit(solution)/shard_map/ppermute | solution.py:18
  381.3 30.3 %collective-permute-start.13 = (bf16[1,6,2,3,64,128]{5,4,3,2,1,0:T(8,128)(2,1)S(1)}, bf16[1,6,2,3,64,128]{5,4,3,2,1,0:T(8,128)(2,1)S(1)}, u32[]{:S(2)}, u32[]{:S(2)}) collective-permute-start(bf16[1,6,2,3,64,128]{5,4,3,2,1,0:T(8,128)(2,1)S(1)} %slice.1612), channel_id=1, source_target_pairs={{16,0},{20,4},{24,8},{28,12},{17,1},{21,5},{25,9},{29,13},{18,2},{... | collective-permute-start | bytes 1769480 | tf_op jit(solution)/shard_map/ppermute | solution.py:18
  382.6 29.6 %collective-permute-start.10 = (bf16[1,6,2,3,64,128]{5,4,3,2,1,0:T(8,128)(2,1)S(1)}, bf16[1,6,2,3,64,128]{5,4,3,2,1,0:T(8,128)(2,1)S(1)}, u32[]{:S(2)}, u32[]{:S(2)}) collective-permute-start(bf16[1,6,2,3,64,128]{5,4,3,2,1,0:T(8,128)(2,1)S(1)} %slice.1612), channel_id=1, source_target_pairs={{0,16},{4,20},{8,24},{12,28},{1,17},{5,21},{9,25},{13,29},{2,18},{... | collective-permute-start | bytes 1769480 | tf_op jit(solution)/shard_map/ppermute | solution.py:18
  411.7 16.3 %collective-permute-start.14 = (bf16[1,6,2,3,64,128]{5,4,3,2,1,0:T(8,128)(2,1)S(1)}, bf16[1,6,2,3,64,128]{5,4,3,2,1,0:T(8,128)(2,1)}, u32[]{:S(2)}, u32[]{:S(2)}) collective-permute-start(bf16[1,6,2,3,64,128]{5,4,3,2,1,0:T(8,128)(2,1)S(1)} %collective-permute-done.13), channel_id=1, source_target_pairs={{0,4},{4,0},{8,12},{12,8},{16,20},{20,16},{24,28},{28,24},{1,5},{5... | collective-permute-start | bytes 1769480 | tf_op jit(solution)/shard_map/ppermute | solution.py:24
  412.2 27.9 %collective-permute-start.11 = (bf16[1,6,2,3,64,128]{5,4,3,2,1,0:T(8,128)(2,1)S(1)}, bf16[1,6,2,3,64,128]{5,4,3,2,1,0:T(8,128)(2,1)}, u32[]{:S(2)}, u32[]{:S(2)}) collective-permute-start(bf16[1,6,2,3,64,128]{5,4,3,2,1,0:T(8,128)(2,1)S(1)} %collective-permute-done.10), channel_id=1, source_target_pairs={{0,4},{4,0},{8,12},{12,8},{16,20},{20,16},{24,28},{28,24},{1,5},{5... | collective-permute-start | bytes 1769480 | tf_op jit(solution)/shard_map/ppermute | solution.py:24
  428.0 47.4 %collective-permute-start.15 = (bf16[1,6,2,3,64,128]{5,4,3,2,1,0:T(8,128)(2,1)}, bf16[1,6,2,3,64,128]{5,4,3,2,1,0:T(8,128)(2,1)}, u32[]{:S(2)}, u32[]{:S(2)}) collective-permute-start(bf16[1,6,2,3,64,128]{5,4,3,2,1,0:T(8,128)(2,1)} %collective-permute-done.14), channel_id=1, source_target_pairs={{0,8},{4,12},{8,0},{12,4},{16,24},{20,28},{24,16},{28,20},{1,9},{5... | collective-permute-start | bytes 1769480 | tf_op jit(solution)/shard_map/ppermute | solution.py:24
  440.1 35.3 %collective-permute-start.12 = (bf16[1,6,2,3,64,128]{5,4,3,2,1,0:T(8,128)(2,1)}, bf16[1,6,2,3,64,128]{5,4,3,2,1,0:T(8,128)(2,1)}, u32[]{:S(2)}, u32[]{:S(2)}) collective-permute-start(bf16[1,6,2,3,64,128]{5,4,3,2,1,0:T(8,128)(2,1)} %collective-permute-done.11), channel_id=1, source_target_pairs={{0,8},{4,12},{8,0},{12,4},{16,24},{20,28},{24,16},{28,20},{1,9},{5... | collective-permute-start | bytes 1769480 | tf_op jit(solution)/shard_map/ppermute | solution.py:24
  475.3 3.6 copy-start.17
  510.1 3.3 copy-start.69
  562.0 3.3 copy-start.69
  (89 other events, 109.8 us)
Sparse Core Ops, SparseCore 0:
  332.7 139.2 all-reduce.3
where the time goes:
time: 593 us; the launch traced here: 590 us
  other arithmetic  167 us (28%)
  waiting for transfers between devices  156 us (26%)
  loops' own time  92.6 us (16%)
  local copies, waits for them, and re-layouts  49.7 us (8%)
  blocking collectives  46.5 us (8%)
  matrix products  31.9 us (5%)
  starting transfers between devices  31.6 us (5%)
  between operations  14.4 us (2%)
    ppermute x8, waiting for transfers between devices, partner(): return lax.ppermute(value, axis, pairs)  63.4 us
    ppermute x8, waiting for transfers between devices, passed_along(): return lax.ppermute(value, axis, pairs)  61.5 us
    another operation x1, loops' own time, local(): lax.scan(first_step, grad_sums, jnp.arange(slot_count))  47.1 us
    psum x1, blocking collectives, local(): lax.psum((grad_sums[0], grad_sums[1], grad_sums[2], grad_sums[3], grad_su...  46.5 us
    another operation x1, loops' own time, local(): outputs = [lax.map(second_step, jnp.arange(slot_count))]  45.5 us
    reduce_sum x6, other arithmetic, kernel_terms(): line_terms.append(jnp.sum(grad_values * window, axis=(0, 1)))  37.4 us
    reduce_sum x2, other arithmetic, layer_rows(): mean_value = jnp.mean(conv_rows, -1, keepdims=True)  35.2 us
    dynamic_update_slice x2, other arithmetic, local(): lax.scan(first_step, grad_sums, jnp.arange(slot_count))  32.2 us
  transfers between devices with their start and end apart: 17, of which 11 were waited for; matrix products, arithmetic and copies ran while one was open for 2% of the time, Pallas kernels for 0%

commit v1 on v0

v1 whole, which is shorter than its diff:
```python
from functools import partial
import math

import jax
import jax.numpy as jnp
from jax import lax
from jax.experimental import pallas as pl
from jax.experimental.pallas import tpu as pltpu
from jax.sharding import PartitionSpec as P

TROWS = 8
EPSILON = 1e-06
BF = jnp.bfloat16
F32 = jnp.float32
MESH = pl.DeviceIdType.MESH
PAIRS = 4
WEST = 5
VMEM_BYTES = 56 * 1024 * 1024


def halo_kernel(per_column, sv, ss, sc, rv, rs, rc, send_sems, recv_sems):
    tile_count = lax.axis_size("tile")
    me = lax.axis_index("tile")
    dp = lax.axis_index("dp")
    columns = tile_count // per_column
    col = me // per_column
    row = me % per_column
    mirror = per_column - 1 - row
    west = (col - 1) * per_column + mirror
    east = (col + 1) * per_column + mirror
    has_prev = row > 0
    has_next = row < per_column - 1
    has_west = col > 0
    has_east = col < columns - 1
    jobs = [
        (has_west, west, ss.at[0], rs.at[1], has_east),
        (has_east, east, ss.at[1], rs.at[0], has_west),
        (has_next, me + 1, sv.at[0], rv.at[0], has_prev),
        (has_prev, me - 1, sv.at[1], rv.at[1], has_next),
        (has_west & has_prev, west + 1, sc.at[0, 0], rc.at[1, 0], has_east & has_prev),
        (has_west & has_next, west - 1, sc.at[0, 1], rc.at[1, 1], has_east & has_next),
        (has_east & has_prev, east + 1, sc.at[1, 0], rc.at[0, 0], has_west & has_prev),
        (has_east & has_next, east - 1, sc.at[1, 1], rc.at[0, 1], has_west & has_next),
    ]
    barrier = pltpu.get_barrier_semaphore()
    for sends, target, _, _, _ in jobs:

        @pl.when(sends)
        def _(target=target):
            pl.semaphore_signal(barrier, inc=1, device_id=(target, dp), device_id_type=MESH)

    peers = sum(sends.astype(jnp.int32) for sends, _, _, _, _ in jobs)
    pl.semaphore_wait(barrier, peers)

    def copy_of(index):
        _, target, source, destination, _ = jobs[index]
        return pltpu.make_async_remote_copy(
            src_ref=source,
            dst_ref=destination,
            send_sem=send_sems.at[index],
            recv_sem=recv_sems.at[index],
            device_id=(target, dp),
            device_id_type=MESH,
        )

    for index in range(len(jobs)):

        @pl.when(jobs[index][0])
        def _(index=index):
            copy_of(index).start()

    for index in range(len(jobs)):

        @pl.when(jobs[index][4])
        def _(index=index):
            copy_of(index).wait_recv()

        @pl.when(jobs[index][0])
        def _(index=index):
            copy_of(index).wait_send()


def exchange(packed, per_column, collective_id):
    any_spec = pl.BlockSpec(memory_space=pl.ANY)
    return pl.pallas_call(
        partial(halo_kernel, per_column),
        out_shape=tuple(jax.ShapeDtypeStruct(part.shape, part.dtype) for part in packed),
        in_specs=[any_spec] * 3,
        out_specs=(any_spec,) * 3,
        scratch_shapes=[pltpu.SemaphoreType.DMA((8,)), pltpu.SemaphoreType.DMA((8,))],
        compiler_params=pltpu.CompilerParams(collective_id=collective_id, has_side_effects=True),
    )(*packed)


def pack(tiles, down):
    extent = tiles.shape[1]
    first, last = tiles[0], tiles[1]
    to_next = jnp.where(down, last[extent - 3 :], last[:3])
    to_prev = jnp.where(down, first[:3], first[extent - 3 :])
    vertical = jnp.stack([to_next, to_prev], 0)
    west = jnp.transpose(tiles[:, :, :3], (0, 2, 1, 3))
    east = jnp.transpose(tiles[:, :, extent - 3 :], (0, 2, 1, 3))
    sides = jnp.stack([west, east], 0)
    low, high = sides[:, :, :, :16], sides[:, :, :, extent - 16 :]
    corner_prev = jnp.where(down, low[:, 0], high[:, 0])
    corner_next = jnp.where(down, high[:, 1], low[:, 1])
    return vertical, sides, jnp.stack([corner_prev, corner_next], 1)


def build_windows(flags, slot, tiles, rv, rs, rc, padded, windows):
    extent = tiles.shape[1]
    width = padded.shape[1]
    down = flags[2, 0] > 0
    first = slot == 0

    def valid(direction, value):
        return jnp.where(flags[slot, direction] > 0, value, jnp.zeros_like(value))

    own = tiles.at[slot]
    other = tiles.at[1 - slot]
    padded[3 : 3 + extent, 8 : 8 + extent, :] = own[...].astype(F32)
    outer = rv[slot].astype(F32)
    inner_is_south = first == down
    inner = jnp.where(inner_is_south, other[:3], other[extent - 3 :]).astype(F32)
    north = jnp.where(inner_is_south, outer, inner)
    south = jnp.where(inner_is_south, inner, outer)
    padded[0:3, 8 : 8 + extent, :] = valid(0, north)
    padded[3 + extent : 6 + extent, 8 : 8 + extent, :] = valid(1, south)
    flat = padded.reshape(padded.shape[0] * width, padded.shape[2])
    for side, base, straight, upper, lower in ((0, WEST, 2, 4, 6), (1, 8 + extent, 3, 5, 7)):
        strips = valid(straight, rs[side, 1 - slot].astype(F32))
        inner_strips = rs[side, slot].astype(F32)
        corner = rc[side, slot].astype(F32)
        above = valid(upper, jnp.where(inner_is_south, corner[:, 13:16], inner_strips[:, extent - 3 :]))
        below = valid(lower, jnp.where(inner_is_south, inner_strips[:, :3], corner[:, 0:3]))
        for column in range(3):
            flat[pl.ds(3 * width + base + column, extent, stride=width), :] = strips[column]
            for line in range(3):
                padded[line, base + column : base + column + 1, :] = above[column, line : line + 1]
                padded[3 + extent + line, base + column : base + column + 1, :] = below[
                    column, line : line + 1
                ]

    def fill(pair, carry):
        for shift in range(7):
            upper_row = padded[2 * pair, WEST + shift : WEST + shift + extent, :]
            lower_row = padded[2 * pair + 1, WEST + shift : WEST + shift + extent, :]
            windows[shift, pair] = jnp.concatenate([upper_row, lower_row], 1).astype(BF)
        return carry

    lax.fori_loop(0, (extent + 6) // 2, fill, 0)


def conv_block(windows, taps, first_pair, pairs):
    extent, lanes = windows.shape[2], windows.shape[3]
    total = None
    for shift in range(7):
        for step in range(4):
            rows = windows[shift, pl.ds(first_pair + step, pairs)].reshape(pairs * extent, lanes)
            term = jnp.dot(rows, taps[shift * 4 + step], preferred_element_type=F32)
            total = term if total is None else total + term
    return total


def split_rows(block):
    pairs = block.shape[0] // 2
    parts = [block[2 * q] for q in range(pairs)] + [block[2 * q + 1] for q in range(pairs)]
    return jnp.concatenate(parts, 0)


def first_kernel(
    flags,
    tiles,
    cot,
    rv,
    rs,
    rc,
    taps,
    vectors,
    w_up,
    up_bias,
    w_down,
    grad_out,
    g_taps,
    g_up,
    g_down,
    g_vec,
    g_hidden,
    padded,
    windows,
    grad_turned,
):
    slot = pl.program_id(0)
    extent, channels = tiles.shape[1], tiles.shape[3]
    lanes = 2 * channels
    rows = PAIRS * extent

    @pl.when(slot == 0)
    def _():
        g_taps[...] = jnp.zeros_like(g_taps)
        g_up[...] = jnp.zeros_like(g_up)
        g_down[...] = jnp.zeros_like(g_down)
        g_vec[...] = jnp.zeros_like(g_vec)
        g_hidden[...] = jnp.zeros_like(g_hidden)

    build_windows(flags, slot, tiles, rv, rs, rc, padded, windows)
    keep = flags[slot, 8] > 0
    conv_bias, ln_gain, ln_bias, layer_scale = (vectors[k : k + 1] for k in range(4))
    root = math.sqrt(2.0 / math.pi)

    def block_step(block, carry):
        total = conv_block(windows, taps, block * PAIRS, PAIRS)
        conv = jnp.concatenate([total[:, :channels], total[:, channels:]], 0) + conv_bias
        cot_rows = split_rows(cot[0, pl.ds(block * 2 * PAIRS, 2 * PAIRS)]).astype(F32)
        cot_rows = jnp.where(keep, cot_rows, jnp.zeros_like(cot_rows))
        centred = conv - jnp.mean(conv, -1, keepdims=True)
        inverse = lax.rsqrt(jnp.mean(centred * centred, -1, keepdims=True) + EPSILON)
        normed = centred * inverse
        scaled = (normed * ln_gain + ln_bias).astype(BF)
        hidden = jnp.dot(scaled, w_up[...], preferred_element_type=F32) + up_bias[...]
        grad_mixed_f = cot_rows * layer_scale
        grad_mixed = grad_mixed_f.astype(BF)
        grad_act = lax.dot_general(
            grad_mixed, w_down[...], (((1,), (1,)), ((), ())), preferred_element_type=F32
        )
        square = hidden * hidden
        gate = 0.5 + 0.5 * jnp.tanh(hidden * (root + (root * 0.044715) * square))
        act_f = hidden * gate
        slope = gate + act_f * (1.0 - gate) * (2.0 * root + (6.0 * root * 0.044715) * square)
        grad_pre_f = grad_act * slope
        activation = act_f.astype(BF)
        grad_pre = grad_pre_f.astype(BF)
        grad_scaled = lax.dot_general(
            grad_pre, w_up[...], (((1,), (1,)), ((), ())), preferred_element_type=F32
        )
        grad_normed = grad_scaled * ln_gain
        grad_conv_f = inverse * (
            grad_normed
            - jnp.mean(grad_normed, -1, keepdims=True)
            - normed * jnp.mean(grad_normed * normed, -1, keepdims=True)
        )
        grad_conv = grad_conv_f.astype(BF)
        for pair in range(PAIRS):
            upper = grad_conv[pair * extent : (pair + 1) * extent]
            lower = grad_conv[rows + pair * extent : rows + (pair + 1) * extent]
            grad_out[0, block * 2 * PAIRS + 2 * pair] = upper
            grad_out[0, block * 2 * PAIRS + 2 * pair + 1] = lower
        both = jnp.concatenate([grad_conv_f[:rows], grad_conv_f[rows:]], 1)
        grad_turned[block] = both.T.astype(BF)
        g_up[...] += lax.dot_general(
            scaled, grad_pre, (((0,), (0,)), ((), ())), preferred_element_type=F32
        )
        g_down[...] += lax.dot_general(
            grad_mixed, activation, (((0,), (0,)), ((), ())), preferred_element_type=F32
        )

        def fold(value):
            return jnp.sum(value.reshape(-1, 8, value.shape[1]), 0)

        g_vec[0] += fold(grad_conv_f)
        g_vec[1] += fold(grad_scaled * normed)
        g_vec[2] += fold(grad_scaled)
        g_vec[3] += fold(cot_rows)
        g_hidden[...] += fold(grad_pre_f)
        return carry

    blocks = extent // (2 * PAIRS)
    lax.fori_loop(0, blocks, block_step, 0)
    line = lax.broadcasted_iota(jnp.int32, (lanes, lanes), 0) % channels
    lane = lax.broadcasted_iota(jnp.int32, (lanes, lanes), 1) % channels

    for shift in range(7):

        def tap_step(step, carry, shift=shift):
            total = None
            for block in range(blocks):
                window = windows[shift, pl.ds(block * PAIRS + step, PAIRS)].reshape(rows, lanes)
                term = jnp.dot(grad_turned[block], window, preferred_element_type=F32)
                total = term if total is None else total + term
            diagonal = jnp.where(line == lane, total, jnp.zeros_like(total))
            even = jnp.sum(diagonal[:channels].reshape(-1, 8, lanes), 0)
            odd = jnp.sum(diagonal[channels:].reshape(-1, 8, lanes), 0)
            g_taps[0, shift * 4 + step] += even
            g_taps[1, shift * 4 + step] += odd
            return carry

        lax.fori_loop(0, 4, tap_step, 0)


def second_kernel(flags, tiles, cot, rv, rs, rc, taps, out, padded, windows):
    slot = pl.program_id(0)
    extent, channels = tiles.shape[1], tiles.shape[3]
    pairs = PAIRS
    build_windows(flags, slot, tiles, rv, rs, rc, padded, windows)
    keep = flags[slot, 8] > 0

    def block_step(block, carry):
        total = conv_block(windows, taps, block * pairs, pairs)
        for pair in range(pairs):
            for half in range(2):
                line = block * 2 * pairs + 2 * pair + half
                part = total[pair * extent : (pair + 1) * extent, half * channels : (half + 1) * channels]
                value = cot[0, line].astype(F32) + part
                out[0, line] = jnp.where(keep, value, jnp.zeros_like(value)).astype(BF)
        return carry

    lax.fori_loop(0, extent // (2 * pairs), block_step, 0)


def tap_matrices(kernel):
    channels = kernel.shape[2]
    by_column = jnp.transpose(kernel, (1, 0, 2)).astype(BF)
    padded = jnp.pad(by_column, ((0, 0), (1, 1), (0, 0)))
    to_even = padded[:, 1:9].reshape(7, 4, 2 * channels)
    to_odd = padded[:, 0:8].reshape(7, 4, 2 * channels)
    row = jnp.arange(2 * channels)
    lane = jnp.arange(2 * channels)
    same = (row[:, None] % channels) == (lane[None, :] % channels)
    values = jnp.where(
        lane[None, None, None, :] < channels, to_even[..., None], to_odd[..., None]
    )
    return jnp.where(same, values, jnp.zeros_like(values)).reshape(28, 2 * channels, 2 * channels)


def whole(shape):
    zeros = (0,) * len(shape)
    return pl.BlockSpec(shape, lambda i: zeros)


def local(
    fields,
    cotangent,
    is_ocean,
    neighbours,
    kernel,
    conv_bias,
    ln_gain,
    ln_bias,
    w_up,
    up_bias,
    w_down,
    down_bias,
    layer_scale,
):
    slots, extent, channels = fields.shape[1], fields.shape[2], fields.shape[4]
    hidden = w_up.shape[1]
    tile_count = lax.axis_size("tile")
    per_column = TROWS // slots
    position = lax.axis_index("tile")
    tiles, cot = fields[0], cotangent[0]

    ids = position * slots + jnp.arange(slots)
    column = ids // TROWS
    west_slot = 2 * TROWS * column - 1 - ids
    east_slot = 2 * TROWS * (column + 1) - 1 - ids
    expected = jnp.stack(
        [ids - 1, ids + 1, west_slot + 1, east_slot + 1, west_slot - 1, east_slot - 1], 1
    )
    upright = jnp.concatenate([neighbours[:, :2], neighbours[:, 4:]], 1)
    down = jnp.any((upright == expected) & (upright >= 0))
    flags = jnp.concatenate(
        [
            jnp.concatenate([(neighbours >= 0).astype(jnp.int32), is_ocean[:, None]], 1),
            jnp.broadcast_to(down.astype(jnp.int32), (1, 9)),
        ],
        0,
    )
    taps = tap_matrices(kernel)
    flipped_taps = tap_matrices(kernel[::-1, ::-1])
    vectors = jnp.stack([conv_bias, ln_gain, ln_bias, layer_scale], 0)

    rv, rs, rc = exchange(pack(tiles, down), per_column, 0)

    smem = pl.BlockSpec(memory_space=pltpu.SMEM)
    one_tile = pl.BlockSpec((1, extent, extent, channels), lambda i: (i, 0, 0, 0))
    padded_width = 16 + extent
    scratch = [
        pltpu.VMEM((extent + 6, padded_width, channels), F32),
        pltpu.VMEM((7, (extent + 6) // 2, extent, 2 * channels), BF),
    ]
    out_shapes = (
        jax.ShapeDtypeStruct(tiles.shape, BF),
        jax.ShapeDtypeStruct((2, 28, 8, 2 * channels), F32),
        jax.ShapeDtypeStruct((channels, hidden), F32),
        jax.ShapeDtypeStruct((channels, hidden), F32),
        jax.ShapeDtypeStruct((4, 8, channels), F32),
        jax.ShapeDtypeStruct((8, hidden), F32),
    )
    operands = (taps, vectors, w_up, up_bias[None], w_down)
    grad_tiles, g_taps, g_up, g_down, g_vec, g_hidden = pl.pallas_call(
        first_kernel,
        grid=(slots,),
        out_shape=out_shapes,
        in_specs=[smem, whole(tiles.shape), one_tile]
        + [whole(part.shape) for part in (rv, rs, rc) + operands],
        out_specs=(one_tile,) + tuple(whole(shape.shape) for shape in out_shapes[1:]),
        scratch_shapes=scratch
        + [pltpu.VMEM((extent // (2 * PAIRS), 2 * channels, PAIRS * extent), BF)],
        compiler_params=pltpu.CompilerParams(vmem_limit_bytes=VMEM_BYTES),
    )(flags, tiles, cot, rv, rs, rc, *operands)

    tap_sums = jnp.sum(g_taps, 2).reshape(2, 7, 8, channels)
    tap_sums = tap_sums[0, :, :7] + tap_sums[1, :, 1:]
    sums = lax.psum(
        (tap_sums, g_up, g_down, jnp.sum(g_vec, 1), jnp.sum(g_hidden, 0)), ("tile", "dp")
    )

    rv, rs, rc = exchange(pack(grad_tiles, down), per_column, 1)
    result = pl.pallas_call(
        second_kernel,
        grid=(slots,),
        out_shape=jax.ShapeDtypeStruct(tiles.shape, BF),
        in_specs=[smem, whole(tiles.shape), one_tile]
        + [whole(part.shape) for part in (rv, rs, rc, flipped_taps)],
        out_specs=one_tile,
        scratch_shapes=scratch,
        compiler_params=pltpu.CompilerParams(vmem_limit_bytes=VMEM_BYTES),
        cost_estimate=pl.CostEstimate(
            flops=2 * slots * extent * extent * 28 * channels * 2 * channels,
            bytes_accessed=8 * 1024 * 1024,
            transcendentals=0,
        ),
    )(flags, grad_tiles, cot, rv, rs, rc, flipped_taps)

    tap_sums, g_up, g_down, g_vec, g_hidden = sums
    scale = 1.0 / math.sqrt(
        fields.shape[0] * lax.axis_size("dp") * slots * tile_count * extent * extent
    )
    g_down = g_down.T
    g_scale = jnp.sum(w_down.astype(F32) * g_down, 0) / layer_scale + down_bias * g_vec[3]
    return (
        result[None],
        jnp.transpose(tap_sums, (1, 0, 2)) * scale,
        g_vec[0] * scale,
        g_vec[1] * scale,
        g_vec[2] * scale,
        g_up * scale,
        g_hidden * scale,
        g_down * scale,
        g_vec[3] * layer_scale * scale,
        g_scale * scale,
    )


def solution(mesh):
    tiled = P("dp", "tile", None, None, None)
    placed = (tiled, tiled, P("tile"), P("tile", None)) + (P(),) * 9
    return jax.shard_map(
        local,
        mesh=mesh,
        in_specs=placed,
        out_specs=(tiled,) + (P(),) * 9,
        check_vma=False,
    )
```

time: 593 us -> 260 us (0.44)
  other arithmetic: 167 us -> 20.9 us
  Pallas kernels: 0 us -> 129 us
  waiting for transfers between devices: 156 us -> 44.6 us
  loops' own time: 92.6 us -> 0 us
  local copies, waits for them, and re-layouts: 49.7 us -> 9.26 us
  matrix products: 31.9 us -> 0 us
  starting transfers between devices: 31.6 us -> 0.04 us
  blocking collectives: 46.5 us -> 40.1 us
    pallas_call x0 -> x4, Pallas kernels: none -> 129 us  [the longest x1 83.9 us: local(): pl.pallas_call(first_kernel, grid=(slots,), out_shape=out_shapes, in_spec...]
    ppermute x16 -> x0, waiting for transfers between devices: 125 us -> none  [the longest x8 63.4 us: partner(): return lax.ppermute(value, axis, pairs)]
    another operation x2 -> x0, loops' own time: 92.6 us -> none  [the longest x1 47.1 us: local(): lax.scan(first_step, grad_sums, jnp.arange(slot_count))]
    reduce_sum x14 -> x4, other arithmetic: 81.3 us -> 1.21 us  [the longest x1 1.06 us: local(): jnp.sum(w_down.astype(F32) * g_down, 0) / layer_scale + down_bias * g_vec[3]]
    dynamic_update_slice x2 -> x0, other arithmetic: 32.2 us -> none  [local(): lax.scan(first_step, grad_sums, jnp.arange(slot_count))]
    dot_general x12 -> x0, matrix products: 31.9 us -> none  [the longest x4 18.5 us: contract_last(): lax.dot_general(left_rows, right_matrix, (((1,), (1,)), ((), ())), prefer...]
    ppermute x16 -> x0, starting transfers between devices: 31.5 us -> none  [the longest x8 27 us: passed_along(): return lax.ppermute(value, axis, pairs)]
    concatenate x8 -> x1, other arithmetic: 16.9 us -> 0.07 us  [local(): jnp.concatenate([(neighbours >= 0).astype(jnp.int32), is_ocean[:, None]], 1)]
  transfers between devices with their start and end apart: 17 -> 1, of which waited for: 11 -> 1; matrix products, arithmetic and copies ran while one was open for 2% -> 4% of each run, Pallas kernels for 0% -> 13%
where the time goes in v1:
time: 260 us; the launch traced here: 259 us
  Pallas kernels  129 us (50%)
  waiting for transfers between devices  44.6 us (17%)
  blocking collectives  40.1 us (15%)
  other arithmetic  20.9 us (8%)
  between operations  15.1 us (6%)
  local copies, waits for them, and re-layouts  9.26 us (4%)
    pallas_call x1, Pallas kernels, local(): pl.pallas_call(first_kernel, grid=(slots,), out_shape=out_shapes, in_spec...  83.9 us
    psum x1, waiting for transfers between devices, local(): lax.psum((tap_sums, g_up, g_down, jnp.sum(g_vec, 1), jnp.sum(g_hidden, 0)...  44.6 us
    psum x1, blocking collectives, local(): lax.psum((tap_sums, g_up, g_down, jnp.sum(g_vec, 1), jnp.sum(g_hidden, 0)...  40.1 us
    pallas_call x1, Pallas kernels, local(): pl.pallas_call(second_kernel, grid=(slots,), out_shape=jax.ShapeDtypeStru...  24.4 us
    pallas_call x2, Pallas kernels, exchange(): pl.pallas_call(partial(halo_kernel, per_column), out_shape=tuple((jax.Sha...  20.9 us
    select_n x1, other arithmetic, tap_matrices(): jnp.where(same, values, jnp.zeros_like(values))  6.57 us
  transfers between devices with their start and end apart: 1, of which 1 were waited for; matrix products, arithmetic and copies ran while one was open for 4% of the time, Pallas kernels for 13%

profile of v1, /device:TPU:0, one launch (start us, length us, event | category | flops | bytes accessed | tf_op | source)
XLA Modules:
  0.0 259.2 jit_solution(9269992806861106226)
XLA Ops:
  7.2 0.0 all-reduce.7.cloned.1.call-start
  7.3 0.8 slice.132
  8.0 0.0 copy-start.5
  8.0 0.0 copy-start.2
  8.0 0.0 copy-start.11
  8.0 3.0 %copy.44 = bf16[1,2,64,64,128]{4,2,3,1,0:T(8,128)(2,1)S(1)} copy(bf16[1,2,64,64,128]{4,3,2,1,0:T(8,128)(2,1)} %param.13) | data formatting | bytes 4194304 | tf_op args[0]
  11.0 0.0 copy-start.6
  11.0 0.0 copy-start.8
  11.0 0.0 copy-start.9
  11.0 0.0 copy-start.10
  11.1 0.1 stack.62
  11.2 0.0 copy-done.5
  11.2 0.7 and_reduce_fusion
  11.9 1.5 select_bitcast_fusion.1
  13.4 0.7 fusion.10
  14.1 0.7 pad_maximum_fusion.ss
  15.4 0.0 copy-done.2
  15.5 0.0 copy-done.11
  15.5 0.1 copy.30
  15.8 0.1 broadcast_compare_fusion
  15.9 0.6 pad_maximum_fusion.4.sc
  16.5 0.7 pad_maximum_fusion.2.sv
  17.2 0.1 pad_add_fusion
  17.2 0.6 concatenate.11.flags
  17.8 11.2 %shard_map.204 = (bf16[2,3,64,128]{3,2,1,0:T(8,128)(2,1)}, bf16[2,2,3,64,128]{4,3,2,1,0:T(8,128)(2,1)}, bf16[2,2,3,16,128]{4,3,2,1,0:T(8,128)(2,1)}) custom-call(bf16[2,3,64,128]{3,2,1,0:T(8,128)(2,1)} %pad_maximum_fusion.2.sv, bf16[2,2,3,64,128]{4,3,2,1,0:T(8,128)(2,1)} %pad_maximum_fusion.ss, bf16[2,2,3,16,128]{4,3,2,1,0:T(8,128)(2,1)} %pad_maximum_fusion.4.sc), custom_call_target="tpu_custom_call" | custom-call | tf_op jit(solution)/shard_map/pallas_call | solution.py:85
  29.1 0.0 copy-done.6
  29.1 0.0 copy-done.8
  29.1 0.0 copy-done.9
  29.1 0.0 copy-done.10
  29.1 0.6 pad_maximum_fusion.6.vectors
  29.7 6.6 %select_select_fusion = (bf16[28,256,256]{2,1,0:T(8,128)(2,1)}, bf16[28,256,256]{2,1,0:T(8,128)(2,1)}) fusion(pred[256]{0:T(512)(128)(4,1)S(1)} %iota_compare_fusion, pred[256,256]{1,0:T(8,128)(4,1)S(1)} %broadcast_compare_fusion, bf16[28,256]{1,0:T(8,128)(2,1)S(1)} %broadcast_in_dim.80, bf16[28,256]{1,0:T(8,128)(2,1)S(1)} %broadcast_in_dim.78, ...), kind=kLoop, calls=%fused_computation | loop fusion | flops 7340032 | bytes 7463168 | tf_op jit(solution)/shard_map/jit(_where)/select_n | solution.py:322
  36.3 83.9 %shard_map.205 = (bf16[2,64,64,128]{3,2,1,0:T(8,128)(2,1)}, f32[2,28,8,256]{3,2,1,0:T(8,128)}, f32[128,512]{1,0:T(8,128)}, f32[128,512]{1,0:T(8,128)}, f32[4,8,128]{2,1,0:T(8,128)}, /*index=5*/f32[8,512]{1,0:T(8,128)}) custom-call(s32[3,9]{1,0:T(4,128)} %concatenate.11.flags, bf16[2,64,64,128]{3,2,1,0:T(8,128)(2,1)} %bitcast.58, ...), custom_call_target="tpu_custom_call" | custom-call | tf_op jit(solution)/shard_map/pallas_call | solution.py:390
  120.1 0.0 all-reduce.7.cloned.1.call-update
  120.2 0.0 copy-start.1
  120.2 0.0 copy-start.4
  120.2 0.0 copy-start.3
  120.2 3.0 %copy.35 = bf16[2,64,64,128]{3,1,2,0:T(8,128)(2,1)S(1)} copy(bf16[2,64,64,128]{3,2,1,0:T(8,128)(2,1)} %get-tuple-element.25.tiles) | data formatting | bytes 4194304 | tf_op jit(solution)/shard_map/pallas_call | solution.py:390
  123.2 0.7 fusion.12
  123.9 0.7 pad_maximum_fusion.1.ss
  124.6 1.5 slice_select_fusion.1
  126.1 0.0 copy-done.1
  126.1 0.1 reduce_sum.36
  126.3 0.0 copy-done.4
  126.3 0.0 copy-done.3
  126.3 40.1 %all-reduce.3 = (f32[7,7,128]{2,1,0:T(8,128)S(1)}, f32[4,128]{1,0:T(4,128)S(1)}, f32[512]{0:T(512)S(1)}) all-reduce(f32[7,7,128]{2,1,0:T(8,128)S(1)} %fusion, f32[4,128]{1,0:T(4,128)S(1)} %reduce_sum.37, f32[512]{0:T(512)S(1)} %reduce_sum.38), channel_id=1, replica_groups=mesh['tile'=8,'dp'=4] {'tile','dp'}, use_global_device_ids=true, to_apply=%region_2.3 | all-reduce | flops 7296 | bytes 58368 | tf_op jit(solution)/shard_map/psum | solution.py:404
  166.4 0.6 pad_maximum_fusion.5.sc
  167.1 0.7 pad_maximum_fusion.3.sv
  167.7 9.7 %shard_map.206 = (bf16[2,3,64,128]{3,2,1,0:T(8,128)(2,1)}, bf16[2,2,3,64,128]{4,3,2,1,0:T(8,128)(2,1)}, bf16[2,2,3,16,128]{4,3,2,1,0:T(8,128)(2,1)}) custom-call(bf16[2,3,64,128]{3,2,1,0:T(8,128)(2,1)} %pad_maximum_fusion.3.sv, bf16[2,2,3,64,128]{4,3,2,1,0:T(8,128)(2,1)} %pad_maximum_fusion.1.ss, bf16[2,2,3,16,128]{4,3,2,1,0:T(8,128)(2,1)} %pad_maximum_fusion.5.sc), custom_call_target="tpu_custom_call" | custom-call | tf_op jit(solution)/shard_map/pallas_call | solution.py:85
  177.4 0.0 copy-start
  177.4 0.0 copy-start.7
  177.4 24.4 %shard_map.207 = bf16[2,64,64,128]{3,2,1,0:T(8,128)(2,1)} custom-call(s32[3,9]{1,0:T(4,128)} %concatenate.11.flags, bf16[2,64,64,128]{3,2,1,0:T(8,128)(2,1)} %get-tuple-element.25.tiles, bf16[2,64,64,128]{3,2,1,0:T(8,128)(2,1)} %bitcast.61, bf16[2,3,64,128]{3,2,1,0:T(8,128)(2,1)} %get-tuple-element.26.rv, bf16[2,2,3,64,128]{4,3,2,1,0:T(8,128)(2,1)} %get-tuple-element.27.rs, ...), custom_call_target="tpu_custom_call" | custom-call | flops 15032385536 | bytes 8388608 | tf_op jit(solution)/shard_map/pallas_call | solution.py:409
  201.8 0.5 multiply_bitcast_fusion.1
  202.4 0.0 copy-done
  202.4 0.1 copy.39
  202.5 0.6 copy.40
  203.1 0.6 broadcast_multiply_fusion.2
  203.7 44.6 %all-reduce.7.cloned.1.call-done = (f32[128,512]{1,0:T(8,128)}, f32[512,128]{0,1:T(8,128)}) async-done(((f32[128,512]{1,0:T(8,128)}, f32[512,128]{0,1:T(8,128)}), (f32[128,512]{1,0:T(8,128)}, f32[512,128]{0,1:T(8,128)})) %all-reduce.7.cloned.1.call-update) | async-done | bytes 524304 | tf_op jit(solution)/shard_map/psum | solution.py:404
  248.3 1.1 multiply_reduce_fusion
  249.3 0.8 copy.41
  250.2 1.7 broadcast_multiply_fusion.1
  251.8 0.0 copy-done.7
  251.8 0.5 fusion.17
  (25 shorter events, 0.2 us)
Async XLA Ops:
  7.2 241.1 %all-reduce.7.cloned.1.call-start = ((), (), s32[]{:S(2)}) async-start(), calls=%async_computation | async-start | bytes 1048576 | tf_op jit(solution)/shard_map/psum | solution.py:404
  8.0 3.1 %copy-start.5 = (s32[2,8]{1,0:T(2,128)S(1)}, s32[2,8]{1,0:T(2,128)}, u32[]{:S(2)}) copy-start(s32[2,8]{1,0:T(2,128)} %param.16) | copy-start | bytes 196
  8.0 7.4 %copy-start.2 = (f32[7,7,128]{2,1,0:T(8,128)S(1)}, f32[7,7,128]{2,1,0:T(8,128)}, u32[]{:S(2)}) copy-start(f32[7,7,128]{2,1,0:T(8,128)} %param.17) | copy-start | bytes 75268
  8.0 7.5 %copy-start.11 = (s32[2]{0:T(128)S(1)}, s32[2]{0:T(128)}, u32[]{:S(2)}) copy-start(s32[2]{0:T(128)} %param.15) | copy-start | bytes 28
  11.0 18.1 %copy-start.6 = (f32[128]{0:T(128)S(1)}, f32[128]{0:T(128)}, u32[]{:S(2)}) copy-start(f32[128]{0:T(128)} %param.25) | copy-start | bytes 1540
  11.0 18.1 %copy-start.8 = (f32[128]{0:T(128)S(1)}, f32[128]{0:T(128)}, u32[]{:S(2)}) copy-start(f32[128]{0:T(128)} %param.20) | copy-start | bytes 1540
  11.0 18.1 %copy-start.9 = (f32[128]{0:T(128)S(1)}, f32[128]{0:T(128)}, u32[]{:S(2)}) copy-start(f32[128]{0:T(128)} %param.19) | copy-start | bytes 1540
  11.0 18.1 %copy-start.10 = (f32[128]{0:T(128)S(1)}, f32[128]{0:T(128)}, u32[]{:S(2)}) copy-start(f32[128]{0:T(128)} %param.18) | copy-start | bytes 1540
  120.2 6.0 %copy-start.1 = (f32[2,28,8,256]{3,2,1,0:T(8,128)S(1)}, f32[2,28,8,256]{3,2,1,0:T(8,128)}, u32[]{:S(2)}) copy-start(f32[2,28,8,256]{3,2,1,0:T(8,128)} %get-tuple-element.29) | copy-start | bytes 1376260
  120.2 6.1 %copy-start.4 = (f32[4,8,128]{2,1,0:T(8,128)S(1)}, f32[4,8,128]{2,1,0:T(8,128)}, u32[]{:S(2)}) copy-start(f32[4,8,128]{2,1,0:T(8,128)} %get-tuple-element.30) | copy-start | bytes 49156
  120.2 6.1 %copy-start.3 = (f32[8,512]{1,0:T(8,128)S(1)}, f32[8,512]{1,0:T(8,128)}, u32[]{:S(2)}) copy-start(f32[8,512]{1,0:T(8,128)} %get-tuple-element.32) | copy-start | bytes 49156
  177.4 25.0 %copy-start = (bf16[512,128]{1,0:T(8,128)(2,1)S(1)}, bf16[512,128]{1,0:T(8,128)(2,1)}, u32[]{:S(2)}) copy-start(bf16[512,128]{1,0:T(8,128)(2,1)} %w_down.1) | copy-start | bytes 393220
  177.4 74.5 %copy-start.7 = (f32[128]{0:T(128)S(1)}, f32[128]{0:T(128)}, u32[]{:S(2)}) copy-start(f32[128]{0:T(128)} %param.24) | copy-start | bytes 1540
Sparse Core Ops, SparseCore 0:
  120.3 127.9 all-reduce.6

commit v2 on v1

--- a/solution.py
+++ b/solution.py
@@ -80,6 +80,91 @@
             copy_of(index).wait_send()
 
 
+def sum_kernel(steps, part, arrived, total, working, send_sems, recv_sems):
+    position = {"tile": lax.axis_index("tile"), "dp": lax.axis_index("dp")}
+    barrier = pltpu.get_barrier_semaphore()
+
+    def partner(axis, stride):
+        bit = (position[axis] // stride) % 2
+        other = dict(position)
+        other[axis] = position[axis] + stride - 2 * stride * bit
+        return bit, (other["tile"], other["dp"])
+
+    for axis, stride in steps:
+        pl.semaphore_signal(
+            barrier, inc=1, device_id=partner(axis, stride)[1], device_id_type=MESH
+        )
+    pl.semaphore_wait(barrier, len(steps))
+    working[...] = part[...]
+    length = part.shape[0]
+    start = 0
+    landing = 0
+    held = []
+    for index, (axis, stride) in enumerate(steps):
+        bit, target = partner(axis, stride)
+        length = length // 2
+        mine = pl.multiple_of(start + bit * length, 8)
+        given = pl.multiple_of(start + (1 - bit) * length, 8)
+        copy = pltpu.make_async_remote_copy(
+            src_ref=working.at[pl.ds(given, length)],
+            dst_ref=arrived.at[pl.ds(landing, length)],
+            send_sem=send_sems.at[index],
+            recv_sem=recv_sems.at[index],
+            device_id=target,
+            device_id_type=MESH,
+        )
+        copy.start()
+        copy.wait()
+        working[pl.ds(mine, length)] = (
+            working[pl.ds(mine, length)] + arrived[pl.ds(landing, length)]
+        )
+        held.append((mine, length, target))
+        start = mine
+        landing += length
+    total[pl.ds(start, length)] = working[pl.ds(start, length)]
+    for index in reversed(range(len(steps))):
+        mine, length, target = held[index]
+        copy = pltpu.make_async_remote_copy(
+            src_ref=total.at[pl.ds(mine, length)],
+            dst_ref=total.at[pl.ds(mine, length)],
+            send_sem=send_sems.at[len(steps) + index],
+            recv_sem=recv_sems.at[len(steps) + index],
+            device_id=target,
+            device_id_type=MESH,
+        )
+        copy.start()
+        copy.wait()
+
+
+def sum_over_devices(part, collective_id):
+    steps = []
+    for axis in ("dp", "tile"):
+        stride = 1
+        while stride < lax.axis_size(axis):
+            steps.append((axis, stride))
+            stride *= 2
+    whole_rows = 8 * 2 ** len(steps)
+    rows = -(-part.shape[0] // whole_rows) * whole_rows
+    part = jnp.pad(part, ((0, rows - part.shape[0]), (0, 0)))
+    shape = jax.ShapeDtypeStruct(part.shape, part.dtype)
+    vmem = pl.BlockSpec(memory_space=pltpu.VMEM)
+    return pl.pallas_call(
+        lambda part, total, arrived, *rest: sum_kernel(steps, part, arrived, total, *rest),
+        out_shape=shape,
+        in_specs=[vmem],
+        out_specs=vmem,
+        scratch_shapes=[
+            pltpu.VMEM(part.shape, part.dtype),
+            pltpu.VMEM(part.shape, part.dtype),
+            pltpu.SemaphoreType.DMA((2 * len(steps),)),
+            pltpu.SemaphoreType.DMA((2 * len(steps),)),
+        ],
+        compiler_params=pltpu.CompilerParams(
+            collective_id=collective_id, has_side_effects=True, vmem_limit_bytes=16 * 1024 * 1024
+        ),
+    )(part)
+
+
 def exchange(packed, per_column, collective_id):
     any_spec = pl.BlockSpec(memory_space=pl.ANY)
     return pl.pallas_call(
@@ -401,10 +486,23 @@
 
     tap_sums = jnp.sum(g_taps, 2).reshape(2, 7, 8, channels)
     tap_sums = tap_sums[0, :, :7] + tap_sums[1, :, 1:]
-    sums = lax.psum(
-        (tap_sums, g_up, g_down, jnp.sum(g_vec, 1), jnp.sum(g_hidden, 0)), ("tile", "dp")
-    )
-
+    strips = hidden // channels
+
+    def stacked(matrix):
+        return jnp.concatenate(
+            [matrix[:, k * channels : (k + 1) * channels] for k in range(strips)], 0
+        )
+
+    def unstacked(rows):
+        return jnp.concatenate(jnp.split(rows, strips, 0), 1)
+
+    parts = [
+        stacked(g_up),
+        stacked(g_down),
+        tap_sums.reshape(49, channels),
+        jnp.sum(g_vec, 1),
+        stacked(jnp.sum(g_hidden, 0)[None]),
+    ]
     rv, rs, rc = exchange(pack(grad_tiles, down), per_column, 1)
     result = pl.pallas_call(
         second_kernel,
@@ -422,7 +520,16 @@
         ),
     )(flags, grad_tiles, cot, rv, rs, rc, flipped_taps)
 
-    tap_sums, g_up, g_down, g_vec, g_hidden = sums
+    sums = sum_over_devices(jnp.concatenate(parts, 0), 2)
+    pieces = []
+    first = 0
+    for part in parts:
+        pieces.append(sums[first : first + part.shape[0]])
+        first += part.shape[0]
+    g_up, g_down = unstacked(pieces[0]), unstacked(pieces[1])
+    tap_sums = pieces[2].reshape(7, 7, channels)
+    g_vec = pieces[3]
+    g_hidden = unstacked(pieces[4])[0]
     scale = 1.0 / math.sqrt(
         fields.shape[0] * lax.axis_size("dp") * slots * tile_count * extent * extent
     )

time: 260 us -> 199 us (0.77)
  waiting for transfers between devices: 44.6 us -> 0 us
  blocking collectives: 40.1 us -> 0 us
  Pallas kernels: 129 us -> 164 us
  between operations: 15.1 us -> 1.59 us
    psum x1 -> x0, waiting for transfers between devices: 44.6 us -> none  [local(): lax.psum((tap_sums, g_up, g_down, jnp.sum(g_vec, 1), jnp.sum(g_hidden, 0)...]
    psum x1 -> x0, blocking collectives: 40.1 us -> none  [local(): lax.psum((tap_sums, g_up, g_down, jnp.sum(g_vec, 1), jnp.sum(g_hidden, 0)...]
    pallas_call x0 -> x1, Pallas kernels: none -> 34.2 us  [sum_over_devices(): pl.pallas_call(lambda part, total, arrived, *rest: sum_kernel(steps, part...]
  transfers between devices with their start and end apart: 1 -> 0, of which waited for: 1 -> 0; matrix products, arithmetic and copies ran while one was open for 4% -> 0% of each run, Pallas kernels for 13% -> 0%
where the time goes in v2:
time: 199 us; the launch traced here: 198 us
  Pallas kernels  164 us (82%)
  other arithmetic  22.1 us (11%)
  local copies, waits for them, and re-layouts  10.3 us (5%)
    pallas_call x1, Pallas kernels, local(): pl.pallas_call(first_kernel, grid=(slots,), out_shape=out_shapes, in_spec...  83.9 us
    pallas_call x1, Pallas kernels, sum_over_devices(): pl.pallas_call(lambda part, total, arrived, *rest: sum_kernel(steps, part...  34.2 us
    pallas_call x1, Pallas kernels, local(): pl.pallas_call(second_kernel, grid=(slots,), out_shape=jax.ShapeDtypeStru...  24.4 us
    pallas_call x2, Pallas kernels, exchange(): pl.pallas_call(partial(halo_kernel, per_column), out_shape=tuple((jax.Sha...  21.4 us
    select_n x1, other arithmetic, tap_matrices(): jnp.where(same, values, jnp.zeros_like(values))  6.65 us

profile of v2, /device:TPU:0, one launch (start us, length us, event | category | flops | bytes accessed | tf_op | source)
XLA Modules:
  0.0 197.9 jit_solution(5751861279615912917)
XLA Ops:
  0.7 0.1 stack.62
  0.8 0.8 slice.191
  1.5 1.4 and_reduce_fusion
  2.9 0.0 copy-start.3
  2.9 0.0 copy-start.9
  3.0 0.0 copy-start.2
  3.0 3.0 %copy.46 = bf16[1,2,64,64,128]{4,2,3,1,0:T(8,128)(2,1)S(1)} copy(bf16[1,2,64,64,128]{4,3,2,1,0:T(8,128)(2,1)} %param.13) | data formatting | bytes 4194304 | tf_op args[0]
  6.0 0.6 fusion.10
  6.6 0.6 pad_maximum_fusion.4.sc
  7.2 1.5 select_bitcast_fusion.1
  8.7 0.7 pad_maximum_fusion.2.sv
  9.4 0.7 pad_maximum_fusion.ss
  10.1 11.2 %shard_map.204 = (bf16[2,3,64,128]{3,2,1,0:T(8,128)(2,1)}, bf16[2,2,3,64,128]{4,3,2,1,0:T(8,128)(2,1)}, bf16[2,2,3,16,128]{4,3,2,1,0:T(8,128)(2,1)}) custom-call(bf16[2,3,64,128]{3,2,1,0:T(8,128)(2,1)} %pad_maximum_fusion.2.sv, bf16[2,2,3,64,128]{4,3,2,1,0:T(8,128)(2,1)} %pad_maximum_fusion.ss, bf16[2,2,3,16,128]{4,3,2,1,0:T(8,128)(2,1)} %pad_maximum_fusion.4.sc), custom_call_target="tpu_custom_call" | custom-call | tf_op jit(solution)/shard_map/pallas_call | solution.py:170
  21.9 0.0 copy-done.3
  21.9 0.0 copy-done.9
  21.9 0.1 copy.31
  22.0 0.1 pad_add_fusion
  22.1 0.5 concatenate.23.flags
  22.6 0.0 copy-done.2
  22.8 0.1 broadcast_compare_fusion
  23.0 0.0 copy-start.4
  23.0 0.0 copy-start.6
  23.0 0.0 copy-start.7
  23.0 0.0 copy-start.8
  23.0 6.6 %select_select_fusion = (bf16[28,256,256]{2,1,0:T(8,128)(2,1)}, bf16[28,256,256]{2,1,0:T(8,128)(2,1)}) fusion(pred[256]{0:T(512)(128)(4,1)S(1)} %iota_compare_fusion, pred[256,256]{1,0:T(8,128)(4,1)S(1)} %broadcast_compare_fusion, bf16[28,256]{1,0:T(8,128)(2,1)S(1)} %broadcast_in_dim.83, bf16[28,256]{1,0:T(8,128)(2,1)S(1)} %broadcast_in_dim.81, ...), kind=kLoop, calls=%fused_computation | loop fusion | flops 7340032 | bytes 7463168 | tf_op jit(solution)/shard_map/jit(_where)/select_n | solution.py:407
  29.7 0.0 copy-done.4
  29.7 0.0 copy-done.6
  29.7 0.0 copy-done.7
  29.7 0.0 copy-done.8
  29.7 0.6 pad_maximum_fusion.6.vectors
  30.3 83.9 %shard_map.205 = (bf16[2,64,64,128]{3,2,1,0:T(8,128)(2,1)}, f32[2,28,8,256]{3,2,1,0:T(8,128)}, f32[128,512]{1,0:T(8,128)}, f32[128,512]{1,0:T(8,128)}, f32[4,8,128]{2,1,0:T(8,128)}, /*index=5*/f32[8,512]{1,0:T(8,128)}) custom-call(s32[3,9]{1,0:T(4,128)} %concatenate.23.flags, bf16[2,64,64,128]{3,2,1,0:T(8,128)(2,1)} %bitcast.64, ...), custom_call_target="tpu_custom_call" | custom-call | tf_op jit(solution)/shard_map/pallas_call | solution.py:475
  114.1 1.0 fusion.20
  115.1 1.0 fusion.21
  116.1 1.1 reduce_sum.36
  117.3 0.7 reduce_sum.38
  118.0 0.7 reduce_sum.37
  118.7 0.0 copy-start.1
  118.7 0.1 concatenate.24
  118.8 0.0 copy-start.5
  118.9 0.0 copy-start
  118.9 34.2 %shard_map.208 = f32[1280,128]{1,0:T(8,128)S(1)} custom-call(f32[1280,128]{1,0:T(8,128)S(1)} %pad.14.part), custom_call_target="tpu_custom_call" | custom-call | tf_op jit(solution)/shard_map/pallas_call | solution.py:151
  153.1 0.7 fusion.18
  153.8 0.0 copy-done.1
  153.8 0.1 copy.41
  153.9 0.1 multiply_reduce_fusion
  154.0 0.0 copy-done.5
  154.0 0.5 fusion.17
  154.6 0.8 copy.42
  155.4 0.5 fusion.19
  155.9 0.6 maximum_multiply_fusion.1
  156.5 1.6 maximum_multiply_fusion
  158.1 0.6 copy.47
  158.7 0.0 copy-done
  158.7 1.4 copy.36
  160.1 0.6 fusion.12
  160.7 0.6 pad_maximum_fusion.5.sc
  161.4 0.7 pad_maximum_fusion.1.ss
  162.1 0.6 slice_select_fusion.1
  162.7 0.6 pad_maximum_fusion.3.sv
  163.3 10.2 %shard_map.206 = (bf16[2,3,64,128]{3,2,1,0:T(8,128)(2,1)}, bf16[2,2,3,64,128]{4,3,2,1,0:T(8,128)(2,1)}, bf16[2,2,3,16,128]{4,3,2,1,0:T(8,128)(2,1)}) custom-call(bf16[2,3,64,128]{3,2,1,0:T(8,128)(2,1)} %pad_maximum_fusion.3.sv, bf16[2,2,3,64,128]{4,3,2,1,0:T(8,128)(2,1)} %pad_maximum_fusion.1.ss, bf16[2,2,3,16,128]{4,3,2,1,0:T(8,128)(2,1)} %pad_maximum_fusion.5.sc), custom_call_target="tpu_custom_call" | custom-call | tf_op jit(solution)/shard_map/pallas_call | solution.py:170
  173.5 24.4 %shard_map.207 = bf16[2,64,64,128]{3,2,1,0:T(8,128)(2,1)} custom-call(s32[3,9]{1,0:T(4,128)} %concatenate.23.flags, bf16[2,64,64,128]{3,2,1,0:T(8,128)(2,1)} %get-tuple-element.25.tiles, bf16[2,64,64,128]{3,2,1,0:T(8,128)(2,1)} %bitcast.67, bf16[2,3,64,128]{3,2,1,0:T(8,128)(2,1)} %get-tuple-element.26.rv, bf16[2,2,3,64,128]{4,3,2,1,0:T(8,128)(2,1)} %get-tuple-element.27.rs, ...), custom_call_target="tpu_custom_call" | custom-call | flops 15032385536 | bytes 8388608 | tf_op jit(solution)/shard_map/pallas_call | solution.py:507
  (27 shorter events, 0.3 us)
Async XLA Ops:
  2.9 19.0 %copy-start.3 = (s32[2,8]{1,0:T(2,128)S(1)}, s32[2,8]{1,0:T(2,128)}, u32[]{:S(2)}) copy-start(s32[2,8]{1,0:T(2,128)} %param.16) | copy-start | bytes 196
  2.9 19.0 %copy-start.9 = (s32[2]{0:T(128)S(1)}, s32[2]{0:T(128)}, u32[]{:S(2)}) copy-start(s32[2]{0:T(128)} %param.15) | copy-start | bytes 28
  3.0 19.7 %copy-start.2 = (f32[7,7,128]{2,1,0:T(8,128)S(1)}, f32[7,7,128]{2,1,0:T(8,128)}, u32[]{:S(2)}) copy-start(f32[7,7,128]{2,1,0:T(8,128)} %param.17) | copy-start | bytes 75268
  23.0 6.7 %copy-start.4 = (f32[128]{0:T(128)S(1)}, f32[128]{0:T(128)}, u32[]{:S(2)}) copy-start(f32[128]{0:T(128)} %param.25) | copy-start | bytes 1540
  23.0 6.7 %copy-start.6 = (f32[128]{0:T(128)S(1)}, f32[128]{0:T(128)}, u32[]{:S(2)}) copy-start(f32[128]{0:T(128)} %param.20) | copy-start | bytes 1540
  23.0 6.7 %copy-start.7 = (f32[128]{0:T(128)S(1)}, f32[128]{0:T(128)}, u32[]{:S(2)}) copy-start(f32[128]{0:T(128)} %param.19) | copy-start | bytes 1540
  23.0 6.7 %copy-start.8 = (f32[128]{0:T(128)S(1)}, f32[128]{0:T(128)}, u32[]{:S(2)}) copy-start(f32[128]{0:T(128)} %param.18) | copy-start | bytes 1540
  118.7 35.1 %copy-start.1 = (bf16[512,128]{1,0:T(8,128)(2,1)S(1)}, bf16[512,128]{1,0:T(8,128)(2,1)}, u32[]{:S(2)}) copy-start(bf16[512,128]{1,0:T(8,128)(2,1)} %w_down.1) | copy-start | bytes 393220
  118.8 35.2 %copy-start.5 = (f32[128]{0:T(128)S(1)}, f32[128]{0:T(128)}, u32[]{:S(2)}) copy-start(f32[128]{0:T(128)} %param.24) | copy-start | bytes 1540
  118.9 39.9 %copy-start = (bf16[2,64,64,128]{3,2,1,0:T(8,128)(2,1)S(1)}, bf16[2,64,64,128]{3,2,1,0:T(8,128)(2,1)}, u32[]{:S(2)}) copy-start(bf16[2,64,64,128]{3,2,1,0:T(8,128)(2,1)} %get-tuple-element.25.tiles) | copy-start | bytes 6291460

commit v3 on v2

--- a/solution.py
+++ b/solution.py
@@ -13,7 +13,7 @@
 BF = jnp.bfloat16
 F32 = jnp.float32
 MESH = pl.DeviceIdType.MESH
-PAIRS = 4
+PAIRS = 8
 WEST = 5
 VMEM_BYTES = 56 * 1024 * 1024
 

time: 199 us -> 193 us (0.970)
  Pallas kernels: 164 us -> 158 us
    pallas_call x1, Pallas kernels: 83.9 us -> 79.4 us  [local(): pl.pallas_call(first_kernel, grid=(slots,), out_shape=out_shapes, in_spec...]
where the time goes in v3:
time: 193 us; the launch traced here: 192 us
  Pallas kernels  158 us (82%)
  other arithmetic  22.1 us (11%)
  local copies, waits for them, and re-layouts  10.3 us (5%)
    pallas_call x1, Pallas kernels, local(): pl.pallas_call(first_kernel, grid=(slots,), out_shape=out_shapes, in_spec...  79.4 us
    pallas_call x1, Pallas kernels, sum_over_devices(): pl.pallas_call(lambda part, total, arrived, *rest: sum_kernel(steps, part...  34.2 us
    pallas_call x1, Pallas kernels, local(): pl.pallas_call(second_kernel, grid=(slots,), out_shape=jax.ShapeDtypeStru...  23 us
    pallas_call x2, Pallas kernels, exchange(): pl.pallas_call(partial(halo_kernel, per_column), out_shape=tuple((jax.Sha...  21.4 us
    select_n x1, other arithmetic, tap_matrices(): jnp.where(same, values, jnp.zeros_like(values))  6.65 us
    unnamed x23, local copies, waits for them, and re-layouts  3.97 us

profile of v3, /device:TPU:0, one launch (start us, length us, event | category | flops | bytes accessed | tf_op | source)
XLA Modules:
  0.0 192.2 jit_solution(14315610044806390723)
XLA Ops:
  0.7 0.1 stack.62
  0.8 0.8 slice.191
  1.5 1.4 and_reduce_fusion
  2.9 0.0 copy-start.3
  2.9 0.0 copy-start.9
  3.0 0.0 copy-start.2
  3.0 3.0 %copy.46 = bf16[1,2,64,64,128]{4,2,3,1,0:T(8,128)(2,1)S(1)} copy(bf16[1,2,64,64,128]{4,3,2,1,0:T(8,128)(2,1)} %param.13) | data formatting | bytes 4194304 | tf_op args[0]
  6.0 0.6 fusion.10
  6.6 0.6 pad_maximum_fusion.4.sc
  7.2 1.5 select_bitcast_fusion.1
  8.7 0.7 pad_maximum_fusion.2.sv
  9.4 0.7 pad_maximum_fusion.ss
  10.1 11.2 %shard_map.204 = (bf16[2,3,64,128]{3,2,1,0:T(8,128)(2,1)}, bf16[2,2,3,64,128]{4,3,2,1,0:T(8,128)(2,1)}, bf16[2,2,3,16,128]{4,3,2,1,0:T(8,128)(2,1)}) custom-call(bf16[2,3,64,128]{3,2,1,0:T(8,128)(2,1)} %pad_maximum_fusion.2.sv, bf16[2,2,3,64,128]{4,3,2,1,0:T(8,128)(2,1)} %pad_maximum_fusion.ss, bf16[2,2,3,16,128]{4,3,2,1,0:T(8,128)(2,1)} %pad_maximum_fusion.4.sc), custom_call_target="tpu_custom_call" | custom-call | tf_op jit(solution)/shard_map/pallas_call | solution.py:170
  21.9 0.0 copy-done.3
  21.9 0.0 copy-done.9
  21.9 0.1 copy.31
  22.0 0.1 pad_add_fusion
  22.1 0.5 concatenate.23.flags
  22.6 0.0 copy-done.2
  22.8 0.1 broadcast_compare_fusion
  23.0 0.0 copy-start.4
  23.0 0.0 copy-start.6
  23.0 0.0 copy-start.7
  23.0 0.0 copy-start.8
  23.0 6.6 %select_select_fusion = (bf16[28,256,256]{2,1,0:T(8,128)(2,1)}, bf16[28,256,256]{2,1,0:T(8,128)(2,1)}) fusion(pred[256]{0:T(512)(128)(4,1)S(1)} %iota_compare_fusion, pred[256,256]{1,0:T(8,128)(4,1)S(1)} %broadcast_compare_fusion, bf16[28,256]{1,0:T(8,128)(2,1)S(1)} %broadcast_in_dim.83, bf16[28,256]{1,0:T(8,128)(2,1)S(1)} %broadcast_in_dim.81, ...), kind=kLoop, calls=%fused_computation | loop fusion | flops 7340032 | bytes 7463168 | tf_op jit(solution)/shard_map/jit(_where)/select_n | solution.py:407
  29.7 0.0 copy-done.4
  29.7 0.0 copy-done.6
  29.7 0.0 copy-done.7
  29.7 0.0 copy-done.8
  29.7 0.6 pad_maximum_fusion.6.vectors
  30.3 79.4 %shard_map.205 = (bf16[2,64,64,128]{3,2,1,0:T(8,128)(2,1)}, f32[2,28,8,256]{3,2,1,0:T(8,128)}, f32[128,512]{1,0:T(8,128)}, f32[128,512]{1,0:T(8,128)}, f32[4,8,128]{2,1,0:T(8,128)}, /*index=5*/f32[8,512]{1,0:T(8,128)}) custom-call(s32[3,9]{1,0:T(4,128)} %concatenate.23.flags, bf16[2,64,64,128]{3,2,1,0:T(8,128)(2,1)} %bitcast.64, ...), custom_call_target="tpu_custom_call" | custom-call | tf_op jit(solution)/shard_map/pallas_call | solution.py:475
  109.7 1.0 fusion.20
  110.7 1.0 fusion.21
  111.7 1.1 reduce_sum.36
  112.8 0.7 reduce_sum.38
  113.6 0.7 reduce_sum.37
  114.3 0.0 copy-start.1
  114.3 0.1 concatenate.24
  114.4 0.0 copy-start.5
  114.5 0.0 copy-start
  114.5 34.2 %shard_map.208 = f32[1280,128]{1,0:T(8,128)S(1)} custom-call(f32[1280,128]{1,0:T(8,128)S(1)} %pad.14.part), custom_call_target="tpu_custom_call" | custom-call | tf_op jit(solution)/shard_map/pallas_call | solution.py:151
  148.7 0.7 fusion.18
  149.4 0.0 copy-done.1
  149.4 0.1 copy.41
  149.5 0.1 multiply_reduce_fusion
  149.6 0.0 copy-done.5
  149.6 0.5 fusion.17
  150.1 0.8 copy.42
  151.0 0.5 fusion.19
  151.5 0.6 maximum_multiply_fusion.1
  152.1 1.6 maximum_multiply_fusion
  153.7 0.6 copy.47
  154.3 0.0 copy-done
  154.3 1.4 copy.36
  155.7 0.6 fusion.12
  156.3 0.6 pad_maximum_fusion.5.sc
  156.9 0.7 pad_maximum_fusion.1.ss
  157.6 0.6 slice_select_fusion.1
  158.3 0.6 pad_maximum_fusion.3.sv
  158.9 10.2 %shard_map.206 = (bf16[2,3,64,128]{3,2,1,0:T(8,128)(2,1)}, bf16[2,2,3,64,128]{4,3,2,1,0:T(8,128)(2,1)}, bf16[2,2,3,16,128]{4,3,2,1,0:T(8,128)(2,1)}) custom-call(bf16[2,3,64,128]{3,2,1,0:T(8,128)(2,1)} %pad_maximum_fusion.3.sv, bf16[2,2,3,64,128]{4,3,2,1,0:T(8,128)(2,1)} %pad_maximum_fusion.1.ss, bf16[2,2,3,16,128]{4,3,2,1,0:T(8,128)(2,1)} %pad_maximum_fusion.5.sc), custom_call_target="tpu_custom_call" | custom-call | tf_op jit(solution)/shard_map/pallas_call | solution.py:170
  169.1 23.0 %shard_map.207 = bf16[2,64,64,128]{3,2,1,0:T(8,128)(2,1)} custom-call(s32[3,9]{1,0:T(4,128)} %concatenate.23.flags, bf16[2,64,64,128]{3,2,1,0:T(8,128)(2,1)} %get-tuple-element.25.tiles, bf16[2,64,64,128]{3,2,1,0:T(8,128)(2,1)} %bitcast.67, bf16[2,3,64,128]{3,2,1,0:T(8,128)(2,1)} %get-tuple-element.26.rv, bf16[2,2,3,64,128]{4,3,2,1,0:T(8,128)(2,1)} %get-tuple-element.27.rs, ...), custom_call_target="tpu_custom_call" | custom-call | flops 15032385536 | bytes 8388608 | tf_op jit(solution)/shard_map/pallas_call | solution.py:507
  (27 shorter events, 0.3 us)
Async XLA Ops:
  2.9 19.0 %copy-start.3 = (s32[2,8]{1,0:T(2,128)S(1)}, s32[2,8]{1,0:T(2,128)}, u32[]{:S(2)}) copy-start(s32[2,8]{1,0:T(2,128)} %param.16) | copy-start | bytes 196
  2.9 19.0 %copy-start.9 = (s32[2]{0:T(128)S(1)}, s32[2]{0:T(128)}, u32[]{:S(2)}) copy-start(s32[2]{0:T(128)} %param.15) | copy-start | bytes 28
  3.0 19.7 %copy-start.2 = (f32[7,7,128]{2,1,0:T(8,128)S(1)}, f32[7,7,128]{2,1,0:T(8,128)}, u32[]{:S(2)}) copy-start(f32[7,7,128]{2,1,0:T(8,128)} %param.17) | copy-start | bytes 75268
  23.0 6.7 %copy-start.4 = (f32[128]{0:T(128)S(1)}, f32[128]{0:T(128)}, u32[]{:S(2)}) copy-start(f32[128]{0:T(128)} %param.25) | copy-start | bytes 1540
  23.0 6.7 %copy-start.6 = (f32[128]{0:T(128)S(1)}, f32[128]{0:T(128)}, u32[]{:S(2)}) copy-start(f32[128]{0:T(128)} %param.20) | copy-start | bytes 1540
  23.0 6.7 %copy-start.7 = (f32[128]{0:T(128)S(1)}, f32[128]{0:T(128)}, u32[]{:S(2)}) copy-start(f32[128]{0:T(128)} %param.19) | copy-start | bytes 1540
  23.0 6.7 %copy-start.8 = (f32[128]{0:T(128)S(1)}, f32[128]{0:T(128)}, u32[]{:S(2)}) copy-start(f32[128]{0:T(128)} %param.18) | copy-start | bytes 1540
  114.3 35.1 %copy-start.1 = (bf16[512,128]{1,0:T(8,128)(2,1)S(1)}, bf16[512,128]{1,0:T(8,128)(2,1)}, u32[]{:S(2)}) copy-start(bf16[512,128]{1,0:T(8,128)(2,1)} %w_down.1) | copy-start | bytes 393220
  114.4 35.2 %copy-start.5 = (f32[128]{0:T(128)S(1)}, f32[128]{0:T(128)}, u32[]{:S(2)}) copy-start(f32[128]{0:T(128)} %param.24) | copy-start | bytes 1540
  114.5 39.9 %copy-start = (bf16[2,64,64,128]{3,2,1,0:T(8,128)(2,1)S(1)}, bf16[2,64,64,128]{3,2,1,0:T(8,128)(2,1)}, u32[]{:S(2)}) copy-start(bf16[2,64,64,128]{3,2,1,0:T(8,128)(2,1)} %get-tuple-element.25.tiles) | copy-start | bytes 6291460
